TPU v7x, 32 devices: a whole 2x2x4 slice. The times are simulated.
32 devices in a mesh: dp: 8 (over z, x), expert: 4 (over y, core).
Axes of the slice: x: 2, y: 2, z: 4, core: 2. Of those that a mesh axis runs over, the one named last changes fastest.
Arguments:
- tokens: bfloat16 [1024, 3072], P('dp', 'expert'), may hold values from -6 to 6
- suffix_cotangent: bfloat16 [512, 3072], P('dp', 'expert'), may hold values from -6 to 6
- prefix_partials: bfloat16 [32, 32, 3072], P('dp', None, 'expert'), may hold values from -6 to 6
- prefix_of_seq: int32 [32], P('dp'), may hold values from 0 to 15
- expert_ids: int32 [1024, 2], P('dp'), may hold values from 0 to 3, all different within a row; in each aligned block of 128 rows (0 to 127, 128 to 255, ...) at most 80 rows name the same one
- router_weight: bfloat16 [3072, 4], P('expert'), may hold values from -0.109375 to 0.109375
- gate_weight: bfloat16 [4, 3072, 8192], P('expert', None, 'dp'), may hold values from -0.109375 to 0.109375
- up_weight: bfloat16 [4, 3072, 8192], P('expert', None, 'dp'), may hold values from -0.109375 to 0.109375
- down_weight: bfloat16 [4, 8192, 3072], P('expert', 'dp'), may hold values from -0.0625 to 0.0625
- gate_pre: bfloat16 [4, 640, 8192], P('expert', None, 'dp'), may hold values from -6 to 6
- up_pre: bfloat16 [4, 640, 8192], P('expert', None, 'dp'), may hold values from -6 to 6
Outputs:
- d_tokens: bfloat16 [1024, 3072], P('dp', 'expert')
- d_gate: bfloat16 [4, 3072, 8192], P('expert', None, 'dp')
- d_up: bfloat16 [4, 3072, 8192], P('expert', None, 'dp')
- d_down: bfloat16 [4, 8192, 3072], P('expert', 'dp')
Inputs may be any that keep to these rules, and one draw needn't show every extreme that they name: `expert_ids`: each row names 2 different experts. Among the rows of one index of dp, each expert is named at most 80 times, a bound that some block reaches. `prefix_of_seq`: block b of the 16 prefix blocks is owned by index b // 2 of dp.
All inputs are finite; a program needn't handle non-finite values.
Results may differ from a plain program's by a relative error of at most 0.025.
Values may be sent and summed in bfloat16 or wider, within the bound.
No kernel may reach another device: no remote copies, remote signals or barrier semaphores. Data moves between devices by JAX's collectives and lax.ppermute only.
A program may use at most 128 MiB of HBM per device.

v0:
```python
import jax
import jax.numpy as jnp
from jax import lax
from jax.sharding import PartitionSpec as P

PREF_DP = 2


def block_sums(prefix_of_seq, prefix_partials, blocks):
    seq_here, block_rows, features = prefix_partials.shape
    owners = (prefix_of_seq[:, None] == jnp.arange(blocks, dtype=jnp.int32)[None, :]).astype(
        jnp.bfloat16
    )
    return jnp.dot(
        owners.T,
        prefix_partials.reshape(seq_here, block_rows * features),
        preferred_element_type=jnp.float32,
    )


def body(
    tokens,
    suffix_cotangent,
    prefix_partials,
    prefix_of_seq,
    expert_ids,
    router_weight,
    gate_weight,
    up_weight,
    down_weight,
    gate_pre,
    up_pre,
):
    dp_count = lax.axis_size("dp")
    tok_rows, features = tokens.shape
    seq_here, block_rows, _ = prefix_partials.shape
    experts = router_weight.shape[1]
    top_count = expert_ids.shape[1]
    row_total = gate_pre.shape[1]
    capacity = row_total // dp_count
    blocks = dp_count * PREF_DP
    local_sum = block_sums(prefix_of_seq, prefix_partials, blocks)
    summed = lax.psum_scatter(
        local_sum.astype(jnp.bfloat16), "dp", scatter_dimension=0, tiled=True
    ).astype(jnp.float32)
    prefix_cot = summed.reshape(PREF_DP * block_rows, features).astype(jnp.bfloat16)
    cot = jnp.concatenate([prefix_cot, suffix_cotangent], axis=0)
    logits = lax.psum(jnp.dot(tokens, router_weight, preferred_element_type=jnp.float32), "expert")
    expert_iota = jnp.arange(experts, dtype=jnp.int32)
    chosen = (expert_ids[:, :, None] == expert_iota[None, None, :]).astype(jnp.float32)
    picked = jnp.sum(logits[:, None, :] * chosen, axis=2)
    first_prob = jax.nn.sigmoid(picked[:, 0] - picked[:, 1])
    second_prob = 1.0 - first_prob
    probs = jnp.stack([first_prob, second_prob], axis=1)
    flat_ids = expert_ids.reshape(-1)
    member = (flat_ids[:, None] == expert_iota[None, :]).astype(jnp.int32)
    before = jnp.cumsum(member, axis=0) - member
    slot_index = jnp.sum(before * member, axis=1)
    target = flat_ids * capacity + slot_index
    placed = target[None, :] == jnp.arange(experts * capacity, dtype=jnp.int32)[:, None]
    routing = jnp.any(placed.reshape(experts * capacity, tok_rows, top_count), axis=2).astype(
        jnp.bfloat16
    )
    send_x = (
        jnp.dot(routing, tokens, preferred_element_type=jnp.float32)
        .astype(jnp.bfloat16)
        .reshape(experts, capacity, features)
    )
    send_g = (
        jnp.dot(routing, cot, preferred_element_type=jnp.float32)
        .astype(jnp.bfloat16)
        .reshape(experts, capacity, features)
    )
    slot_weights = (
        jnp.sum(jnp.where(placed, probs.reshape(-1)[None, :], 0.0), axis=1)
        .astype(jnp.bfloat16)
        .reshape(experts, capacity)
    )
    my_expert = lax.axis_index("expert")
    gate_w = gate_weight[0]
    up_w = up_weight[0]
    down_w = down_weight[0]
    gate_saved = gate_pre[0]
    up_saved = up_pre[0]
    rows_x, rows_g = (
        lax.all_to_all(send_x, "expert", split_axis=0, concat_axis=2, tiled=True),
        lax.all_to_all(send_g, "expert", split_axis=0, concat_axis=2, tiled=True),
    )
    mine_weight = lax.dynamic_index_in_dim(slot_weights, my_expert, 0, keepdims=False)
    piece_x = lax.all_gather(rows_x[0], "dp", axis=0, tiled=True)
    piece_g = lax.all_gather(rows_g[0], "dp", axis=0, tiled=True)
    piece_weight = lax.all_gather(mine_weight, "dp", axis=0, tiled=True)
    gate_act = gate_saved.astype(jnp.float32)
    up_act = up_saved.astype(jnp.float32)
    sigmoid_a = jax.nn.sigmoid(gate_act)
    activation = gate_act * sigmoid_a
    slope = sigmoid_a * (1.0 + gate_act * (1.0 - sigmoid_a))
    hidden = activation * up_act
    d_hidden = lax.dot_general(
        piece_g, down_w, (((1,), (1,)), ((), ())), preferred_element_type=jnp.float32
    )
    dots_piece = jnp.sum(hidden * d_hidden, axis=1)
    weight_col = piece_weight.astype(jnp.float32)[:, None]
    scaled = weight_col * d_hidden
    weighted = (weight_col * hidden).astype(jnp.bfloat16)
    d_gate_act = (scaled * up_act * slope).astype(jnp.bfloat16)
    d_up_act = (scaled * activation).astype(jnp.bfloat16)
    grad_down = lax.dot_general(
        weighted, piece_g, (((0,), (0,)), ((), ())), preferred_element_type=jnp.float32
    )
    grad_gate = lax.dot_general(
        piece_x, d_gate_act, (((0,), (0,)), ((), ())), preferred_element_type=jnp.float32
    )
    grad_up = lax.dot_general(
        piece_x, d_up_act, (((0,), (0,)), ((), ())), preferred_element_type=jnp.float32
    )
    dx_piece = lax.dot_general(
        d_gate_act, gate_w, (((1,), (1,)), ((), ())), preferred_element_type=jnp.float32
    )
    dx_piece = dx_piece + lax.dot_general(
        d_up_act, up_w, (((1,), (1,)), ((), ())), preferred_element_type=jnp.float32
    )
    dx_rows = dx_piece
    dots = dots_piece
    result = (grad_down, grad_gate, grad_up, dx_rows, dots)
    grad_down, grad_gate, grad_up, dx_rows, dots = result
    returned = lax.psum_scatter(
        dx_rows.astype(jnp.bfloat16), "dp", scatter_dimension=0, tiled=True
    ).astype(jnp.float32)
    slot_dots = lax.psum_scatter(dots, "dp", scatter_dimension=0, tiled=True)
    spread = jnp.broadcast_to(slot_dots[None, :, None], (1, capacity, experts))
    rows_in, dots_in = (
        lax.all_to_all(
            returned[None].astype(jnp.bfloat16), "expert", split_axis=2, concat_axis=0, tiled=True
        ).astype(jnp.float32),
        lax.all_to_all(
            spread.astype(jnp.bfloat16), "expert", split_axis=2, concat_axis=0, tiled=True
        ).astype(spread.dtype),
    )
    pair_rows = jnp.take(rows_in.reshape(experts * capacity, features), target, axis=0).reshape(
        tok_rows, top_count, features
    )
    dx_experts = pair_rows[:, 0] + pair_rows[:, 1]
    pair_dots = jnp.take(dots_in.reshape(-1), target).reshape(tok_rows, top_count)
    d_logit = first_prob * second_prob * (pair_dots[:, 0] - pair_dots[:, 1])
    d_logits = d_logit[:, None] * (chosen[:, 0, :] - chosen[:, 1, :])
    dx_router = jnp.dot(
        d_logits, router_weight.astype(jnp.float32).T, precision=lax.Precision.HIGHEST
    )
    d_tokens = (dx_experts + dx_router).astype(jnp.bfloat16)
    return (
        d_tokens,
        grad_gate.astype(jnp.bfloat16)[None],
        grad_up.astype(jnp.bfloat16)[None],
        grad_down.astype(jnp.bfloat16)[None],
    )


def solution(mesh):
    return jax.shard_map(
        body,
        mesh=mesh,
        in_specs=(
            P("dp", "expert"),
            P("dp", "expert"),
            P("dp", None, "expert"),
            P("dp"),
            P("dp", None),
            P("expert", None),
            P("expert", None, "dp"),
            P("expert", None, "dp"),
            P("expert", "dp", None),
            P("expert", None, "dp"),
            P("expert", None, "dp"),
        ),
        out_specs=(
            P("dp", "expert"),
            P("expert", None, "dp"),
            P("expert", None, "dp"),
            P("expert", "dp", None),
        ),
        check_vma=False,
    )
```

profile of v0, /device:TPU:0, one launch (start us, length us, event | category | flops | bytes accessed | tf_op | source)
XLA Modules:
  0.0 381.9 jit_solution(17362727162658212890)
XLA Ops:
  7.2 1.1 copy.75
  8.4 2.1 convolution_convert_fusion
  10.5 0.8 copy.61
  11.3 0.1 eq.72
  11.4 0.1 reshape.141
  11.6 1.2 reduce-window.6
  12.8 0.1 slice.44
  12.9 0.1 copy.63
  13.0 0.1 copy.64
  13.1 0.1 add_bitcast_fusion
  13.2 0.1 reduce_sum.41
  13.4 0.1 copy.65
  13.4 1.3 fusion.35
  15.4 0.7 broadcast_multiply_fusion
  16.2 73.3 %all-reduce.5.cloned.1.call-done = bf16[16,24576]{1,0:T(8,128)(2,1)} async-done(((bf16[16,24576]{1,0:T(8,128)(2,1)}), bf16[16,24576]{1,0:T(8,128)(2,1)}) %all-reduce.5.cloned.1.call-update) | async-done | bytes 786448
  89.5 1.1 constant_dynamic-slice_fusion
  90.6 0.1 convert_element_type.119
  90.6 0.3 convolution_convert_fusion.2
  90.9 11.0 %all_to_all.48 = bf16[4,80,768]{2,1,0:T(8,128)(2,1)S(1)} all-to-all(bf16[4,80,768]{2,1,0:T(8,128)(2,1)S(1)} %bitcast.123), channel_id=1, replica_groups=mesh['dp'=8,'expert'=4] {'expert'}, dimensions={0} | all-to-all | bytes 983040 | tf_op jit(solution)/shard_map/all_to_all | solution.py:87
  102.0 0.3 copy.67
  102.2 0.8 copy.76
  103.1 0.3 convolution_convert_fusion.1
  103.4 10.9 %all_to_all.49 = bf16[4,80,768]{2,1,0:T(8,128)(2,1)S(1)} all-to-all(bf16[4,80,768]{2,1,0:T(8,128)(2,1)S(1)} %bitcast.126), channel_id=1, replica_groups=mesh['dp'=8,'expert'=4] {'expert'}, dimensions={0} | all-to-all | bytes 983040 | tf_op jit(solution)/shard_map/all_to_all | solution.py:86
  114.3 0.3 copy.73
  114.6 0.8 copy.77
  116.1 0.1 copy.70
  116.2 0.1 mul.111
  116.3 0.1 fusion.36
  116.5 6.1 %psum.7 = f32[128,4]{0,1:T(4,128)S(1)} all-reduce(f32[128,4]{0,1:T(4,128)S(1)} %fusion.36), channel_id=1, replica_groups=mesh['dp'=8,'expert'=4] {'expert'}, use_global_device_ids=true, to_apply=%region_3.0 | all-reduce | flops 512 | bytes 4096 | tf_op jit(solution)/shard_map/psum | solution.py:48
  122.6 49.0 %all-gather.4.cloned.1.call-done = bf16[640,3072]{1,0:T(8,128)(2,1)} async-done(((bf16[80,3072]{1,0:T(8,128)(2,1)}), bf16[640,3072]{1,0:T(8,128)(2,1)}) %all-gather.4.cloned.1.call-update) | async-done | bytes 3932176 | tf_op jit(solution)/shard_map/all_gather | solution.py:91
  171.6 9.3 %multiply_reduce_fusion = (f32[640]{0:T(1024)S(1)}, f32[640,1024]{1,0:T(8,128)S(1)}) fusion(bf16[1,640,1024]{2,1,0:T(8,128)(2,1)} %param.21, bf16[1,640,1024]{2,1,0:T(8,128)(2,1)} %param.20, bf16[640,3072]{1,0:T(8,128)(2,1)} %all-gather.4.cloned.1.call-done, bf16[1,1024,3072]{2,1,0:T(8,128)(2,1)} %param.19), kind=kOutput, calls=%fused_computation.26 | convolution fusion | flops 4032429568 | bytes 15469056 | tf_op jit(solution)/shard_map/dot_general | solution.py:99
  180.9 19.2 %all-reduce.2 = bf16[640]{0:T(1024)(128)(2,1)S(1)} all-reduce(f32[640]{0:T(1024)S(1)} %get-tuple-element.12), channel_id=5, replica_groups=mesh['dp'=8,'expert'=4] {'dp'}, use_global_device_ids=true, to_apply=%region_10.11.clone | all-reduce | flops 640 | bytes 3840
  200.0 0.1 dynamic-slice.7
  200.1 0.6 broadcast_in_dim.61
  200.7 3.2 all-to-all-start.2
  204.6 2.9 all-to-all-done.2
  207.6 0.1 reshape.149
  207.7 1.9 gather_fusion.1
  209.6 0.1 gather.15
  209.9 0.1 copy.66
  210.0 0.1 broadcast_in_dim.57
  210.1 0.2 select_reduce_fusion
  210.3 0.1 convert_element_type.116
  210.4 0.2 dynamic-update-slice
  210.6 18.3 %all-reduce = bf16[640]{0:T(1024)(128)(2,1)S(1)} all-reduce(bf16[640]{0:T(1024)(128)(2,1)S(1)} %dynamic-update-slice), channel_id=2, replica_groups=mesh['dp'=8,'expert'=4] {'dp'}, use_global_device_ids=true, to_apply=%add | all-reduce | flops 640 | bytes 2560
  229.0 3.3 fusion.9
  232.3 10.3 %fusion = f32[640,3072]{1,0:T(8,128)} fusion(bf16[1,3072,1024]{2,1,0:T(8,128)(2,1)} %param.18, f32[640,1024]{1,0:T(8,128)S(1)} %get-tuple-element.13, f32[640]{0:T(1024)S(1)} %convert_element_type.154, bf16[1,640,1024]{2,1,0:T(8,128)(2,1)S(1)} %copy-done.2), kind=kOutput, calls=%fused_computation.4 | convolution fusion | flops 4031774720 | bytes 18090496 | tf_op jit(solution)/shard_map/dot_general | solution.py:120
  242.7 8.0 %add_convert_fusion = bf16[640,3072]{1,0:T(8,128)(2,1)} fusion(f32[640,3072]{1,0:T(8,128)} %fusion, bf16[640,1024]{1,0:T(8,128)(2,1)S(1)} %fusion.9, bf16[1,3072,1024]{2,1,0:T(8,128)(2,1)S(1)} %bitcast.137), kind=kOutput, calls=%fused_computation.3 | convolution fusion | flops 4030464000 | bytes 19398656 | tf_op jit(solution)/shard_map/dot_general | solution.py:117
  250.7 9.8 %convert_bitcast_fusion = bf16[1,1024,3072]{2,1,0:T(8,128)(2,1)} fusion(bf16[640,3072]{1,0:T(8,128)(2,1)} %all-gather.4.cloned.1.call-done, bf16[1,640,1024]{2,1,0:T(8,128)(2,1)} %param.21, f32[640]{0:T(1024)S(1)} %convert_element_type.154, bf16[1,640,1024]{2,1,0:T(8,128)(2,1)} %param.20), kind=kOutput, calls=%fused_computation.10 | convolution fusion | flops 4035575808 | bytes 12847616 | tf_op jit(solution)/shard_map/dot_general | solution.py:108
  260.5 9.7 %convert_bitcast_fusion.1 = bf16[1,3072,1024]{2,1,0:T(8,128)(2,1)} fusion(bf16[640,3072]{1,0:T(8,128)(2,1)} %all-gather.6.cloned.1.call-done, f32[640,1024]{1,0:T(8,128)S(1)} %get-tuple-element.13, f32[640]{0:T(1024)S(1)} %convert_element_type.154, bf16[1,640,1024]{2,1,0:T(8,128)(2,1)} %param.20), kind=kOutput, calls=%fused_computation.11 | convolution fusion | flops 4034920448 | bytes 14158336 | tf_op jit(solution)/shard_map/dot_general | solution.py:114
  270.2 62.2 %reduce-scatter.2.cloned.1.call-done = bf16[80,3072]{1,0:T(8,128)(2,1)} async-done(((bf16[640,3072]{1,0:T(8,128)(2,1)}), bf16[80,3072]{1,0:T(8,128)(2,1)}) %reduce-scatter.2.cloned.1.call-update) | async-done | bytes 491536 | tf_op jit(solution)/shard_map/reduce_scatter | solution.py:127
  332.4 3.6 copy.68
  336.1 0.5 broadcast.129
  336.6 17.2 %reduce = bf16[3072,80]{1,0:T(8,128)(2,1)S(1)} reduce(bf16[3072,1,80]{2,1,0:T(2,128)(2,1)S(1)} %bitcast.119, bf16[]{:T(256)} %broadcast.129), dimensions={1}, to_apply=%bitcast.100.reduce_sub_computation | reduce | bytes 983042
  353.8 2.2 reshape.179
  356.0 3.5 all-to-all-start.1
  359.5 9.3 %convert_bitcast_fusion.2 = bf16[1,3072,1024]{2,1,0:T(8,128)(2,1)} fusion(bf16[640,3072]{1,0:T(8,128)(2,1)} %all-gather.6.cloned.1.call-done, bf16[640,1024]{1,0:T(8,128)(2,1)} %copy-done.3), kind=kOutput, calls=%fused_computation.12 | convolution fusion | flops 4029677568 | bytes 11534336 | tf_op jit(solution)/shard_map/dot_general | solution.py:111
  368.8 1.6 reshape.180
  370.4 1.7 bitcast_convert_fusion
  372.1 0.5 copy.69
  372.6 1.1 gather_fusion
  373.7 0.5 gather.13
  374.2 0.1 copy_select_fusion
  374.3 1.1 fusion.17
  (48 shorter events, 0.6 us)
Async XLA Ops:
  7.2 96.0 %copy-start = (bf16[128,768]{1,0:T(8,128)(2,1)S(1)}, bf16[128,768]{1,0:T(8,128)(2,1)}, u32[]{:S(2)}) copy-start(bf16[128,768]{1,0:T(8,128)(2,1)} %param.11) | copy-start | bytes 589828
  7.2 83.5 %copy-start.4 = (bf16[64,768]{1,0:T(8,128)(2,1)S(1)}, bf16[64,768]{1,0:T(8,128)(2,1)}, u32[]{:S(2)}) copy-start(bf16[64,768]{1,0:T(8,128)(2,1)} %param.12) | copy-start | bytes 294916
  7.2 82.3 %all-reduce.5.cloned.1.call-start = ((), (), s32[]{:S(2)}) async-start(), calls=%async_computation.8 | async-start | bytes 1572864
  10.4 161.1 %all-gather.4.cloned.1.call-start = ((), (), s32[]{:S(2)}) async-start(), calls=%async_computation.5 | async-start | bytes 4423680 | tf_op jit(solution)/shard_map/all_gather | solution.py:91
  103.1 13.3 %copy-start.5 = (bf16[768,4]{0,1:T(4,128)(2,1)S(1)}, bf16[768,4]{0,1:T(4,128)(2,1)}, u32[]{:S(2)}) copy-start(bf16[768,4]{0,1:T(4,128)(2,1)} %param.16) | copy-start | bytes 18436
  103.1 19.5 %copy-start.6 = (s32[128,2]{0,1:T(2,128)S(1)}, s32[128,2]{0,1:T(2,128)}, u32[]{:S(2)}) copy-start(s32[128,2]{0,1:T(2,128)} %param.15) | copy-start | bytes 3076
  103.1 157.4 %all-gather.6.cloned.1.call-start = ((), (), s32[]{:S(2)}) async-start(), calls=%async_computation.7 | async-start | bytes 4423680 | tf_op jit(solution)/shard_map/all_gather | solution.py:90
  200.7 6.9 %all-to-all-start.2 = ((bf16[1,80,4]{1,0,2:T(2,128)(2,1)}), bf16[1,80,4]{1,0,2:T(2,128)(2,1)S(1)}, u32[]{:S(2)}, u32[]{:S(2)}) async-start(bf16[1,80,4]{1,0,2:T(2,128)(2,1)} %broadcast_in_dim.61), calls=%async_computation.3 | async-start | bytes 4096 | tf_op jit(solution)/shard_map/all_to_all | solution.py:136
  203.9 128.5 %reduce-scatter.2.cloned.1.call-start = ((), (), s32[]{:S(2)}) async-start(), calls=%async_computation.6 | async-start | bytes 4423680 | tf_op jit(solution)/shard_map/reduce_scatter | solution.py:127
  229.0 3.3 copy-start.2
  229.0 13.7 %slice-start = ((s8[6291456]{0:T(1024)(128)(4,1)}), s8[4194304]{0:T(1024)(128)(4,1)S(1)}, s32[]{:S(2)}) async-start(s8[6291456]{0:T(1024)(128)(4,1)} %bitcast.136), calls=%async_computation.9 | async-start | bytes 8388608
  232.3 10.4 %copy-start.3 = (bf16[640,1024]{1,0:T(8,128)(2,1)}, bf16[640,1024]{1,0:T(8,128)(2,1)S(1)}, u32[]{:S(2)}) copy-start(bf16[640,1024]{1,0:T(8,128)(2,1)S(1)} %fusion.9) | copy-start | bytes 3932164
  232.3 10.4 %slice-start.1 = ((s8[6291456]{0:T(1024)(128)(4,1)}), s8[2097152]{0:T(1024)(128)(4,1)S(1)}, s32[]{:S(2)}) async-start(s8[6291456]{0:T(1024)(128)(4,1)} %bitcast.136), calls=%async_computation.10 | async-start | bytes 4194304
  356.0 12.8 %all-to-all-start.1 = ((bf16[4,2,30720]{2,1,0:T(2,128)(2,1)}), bf16[4,2,30720]{2,1,0:T(2,128)(2,1)S(1)}, u32[]{:S(2)}, u32[]{:S(2)}) async-start(bf16[4,2,30720]{2,1,0:T(2,128)(2,1)} %reshape.179), calls=%async_computation.2 | async-start | bytes 983040 | tf_op jit(solution)/shard_map/all_to_all | solution.py:133
  372.6 2.8 copy-start.1
Sparse Core Ops, SparseCore 0:
  12.0 77.3 all-reduce.4
  103.2 68.3 all-gather.3
  174.6 69.3 all-gather.5
  250.8 81.6 reduce-scatter.1
where the time goes:
time: 383 us; the launch traced here: 382 us
  waiting for transfers between devices  187 us (49%)
  blocking collectives  65.5 us (17%)
  matrix products  60.2 us (16%)
  other arithmetic  24.6 us (6%)
  local copies, waits for them, and re-layouts  21.1 us (6%)
  between operations  16.1 us (4%)
  starting transfers between devices  6.85 us (2%)
    unnamed x5, waiting for transfers between devices  73.4 us
    reduce_scatter x1, waiting for transfers between devices, body(): lax.psum_scatter(dx_rows.astype(jnp.bfloat16), 'dp', scatter_dimension=0,...  62.2 us
    all_gather x1, waiting for transfers between devices, body(): piece_g = lax.all_gather(rows_g[0], 'dp', axis=0, tiled=True)  49 us
    unnamed x2, blocking collectives  37.5 us
    unnamed x3, other arithmetic  17.3 us
    all_to_all x1, blocking collectives, body(): lax.all_to_all(send_g, 'expert', split_axis=0, concat_axis=2, tiled=True)  11 us
    all_to_all x1, blocking collectives, body(): lax.all_to_all(send_x, 'expert', split_axis=0, concat_axis=2, tiled=True)  10.9 us
    unnamed x31, local copies, waits for them, and re-layouts  10.7 us
  transfers between devices with their start and end apart: 6, of which 4 were waited for; matrix products, arithmetic and copies ran while one was open for 18% of the time, Pallas kernels for 0%

commit v1 on v0

v1 whole, which is shorter than its diff:
```python
import functools

import jax
import jax.numpy as jnp
from jax import lax
from jax.experimental import pallas as pl
from jax.experimental.pallas import tpu as pltpu
from jax.sharding import PartitionSpec as P

PREF_DP = 2
AXES = ("dp", "expert")
F32, BF16 = jnp.float32, jnp.bfloat16
MIB = 1 << 20
GFLOP = 10**9
X, Z1, Z2, Y, C = (1, 0), (2, 0), (4, 0), (0, 2), (0, 1)


def xor(a, b):
    return a[0] ^ b[0], a[1] ^ b[1]


def send(value, mask):
    dps, experts = lax.axis_size("dp"), lax.axis_size("expert")
    pairs = [
        (d * experts + e, (d ^ mask[0]) * experts + (e ^ mask[1]))
        for d in range(dps)
        for e in range(experts)
    ]
    return lax.ppermute(value, AXES, pairs)


def bits(count, start):
    return [1 << b for b in range(start, count.bit_length() - 1)]


TREE = [
    (Z2, (0, 0)),
    (X, (0, 0)),
    (Y, (0, 0)),
    (Z1, (0, 0)),
    (Y, (1, 0)),
    (Z1, (0, 2)),
    (X, (4, 0)),
    (Y, (4, 0)),
    (Z1, (4, 0)),
    (X, (2, 0)),
    (Y, (5, 0)),
    (Z1, (4, 2)),
    (X, (6, 0)),
    (Y, (3, 0)),
    (Z1, (5, 2)),
]
X_AT = (5, 0)
SMALL_AT = ((2, 0), (4, 0), (6, 0), (6, 2))


def whole_extra(rows):
    base = rows[None, None]
    for bit in bits(lax.axis_size("dp"), 3):
        base = jnp.concatenate([base, send(base, (bit, 0))], axis=1)
    for bit in bits(lax.axis_size("expert"), 2):
        base = jnp.concatenate([base, send(base, (0, bit))], axis=0)
    return base


def gather_tree(rows):
    pieces = {(0, 0): whole_extra(rows)}
    for link, mask in TREE:
        pieces[xor(link, mask)] = send(pieces[mask], link)
    return pieces


def gather_column(rows, token):
    base, _ = lax.optimization_barrier((whole_extra(rows), token))
    two, one = send(base, Z2), send(base, Z1)
    return jnp.stack([base, one, two, send(two, Z1)])


class SmallGather:
    def __init__(self, logits, router_t, rest):
        self.logits, self.routers, self.rest, self.whole = logits, router_t, rest, None
        self.todo = [(0, bit) for bit in bits(lax.axis_size("expert"), 0)]
        self.todo += [(bit, 0) for bit in bits(lax.axis_size("dp"), 0)]

    def step(self, token=None):
        mask = self.todo.pop(0)
        experts, tok = self.logits.shape
        if mask[1]:
            wide = jnp.pad(self.logits, ((0, 0), (0, self.routers.shape[1] - tok)))
            mine = jnp.concatenate([wide, self.routers], axis=0)
        else:
            if self.whole is None:
                whole = jnp.concatenate([self.logits, self.rest], axis=0)
                self.whole = jnp.pad(whole, ((0, -whole.shape[0] % 8), (0, 0)))[None]
            mine = self.whole
        if token is not None:
            mine, _ = lax.optimization_barrier((mine, token))
        other = send(mine, mask)
        if mask[1]:
            self.logits = self.logits + other[:experts, :tok]
            self.routers = jnp.concatenate([self.routers, other[experts:]], axis=0)
        else:
            self.whole = jnp.concatenate([mine, other], axis=0)

    def finish(self):
        while self.todo:
            self.step()
        return self.whole, self.routers.reshape(-1, self.logits.shape[0], self.routers.shape[1])


def route_g_kernel(sizes, my_ref, pid_ref, *refs):
    dps, cap, pblk, seqs, suf = sizes
    pieces, routing = refs[:8], refs[8]
    out, away, sums = refs[-3:]
    features = sums.shape[-1]
    sums[...] = jnp.zeros_like(sums)
    for md in range(dps):
        group = my_ref[0] ^ md
        for s in range(seqs):
            block = pid_ref[group * seqs + s]
            low = suf + s * pblk
            sums[block] += pieces[md % 8][0, 0, md // 8, low : low + pblk, :].astype(F32)
    for md in range(dps):
        group = my_ref[0] ^ md
        prefix = sums[pl.ds(group * PREF_DP, PREF_DP)].reshape(PREF_DP * pblk, features)
        cot = jnp.concatenate([prefix.astype(BF16), pieces[md % 8][0, 0, md // 8, :suf]], axis=0)
        both = jnp.dot(routing[group], cot, preferred_element_type=F32).astype(BF16)
        out[group] = both[:cap]
        away[group] = both[cap:]


def route_x_kernel(sizes, my_ref, pid_ref, *refs):
    dps, cap = sizes[:2]
    pieces, routing = refs[:8], refs[8]
    out, away = refs[-2:]
    for md in range(dps):
        group = my_ref[0] ^ md
        both = jnp.dot(routing[group], pieces[md % 8][0, 0, md // 8], preferred_element_type=F32).astype(BF16)
        out[group] = both[:cap]
        away[group] = both[cap:]


def route(pieces, y, k, my_dp, my_e, prefix_ids, routing, prior, sizes):
    dps, twice_cap, tok = routing.shape
    cap = twice_cap // 2
    eights = [pieces[md, y] for md in range(8)]
    _, _, ex_dp, rows, features = eights[0][0].shape
    n_e = lax.axis_size("expert")
    scalars = jnp.stack([my_dp, my_e ^ (2 * y + 4 * k)]).astype(jnp.int32)
    block = pl.BlockSpec((dps, cap, features), lambda i, my, pid: (0, 0, my[1]))
    in_specs = [
        pl.BlockSpec((1, 1, ex_dp, rows, features), lambda i, my, pid, at=at: (at, k, 0, 0, 0))
        for _, at in eights
    ]
    in_specs += [pl.BlockSpec((dps, twice_cap, tok), lambda i, my, pid: (0, 0, 0))]
    operands = [*(piece for piece, _ in eights), routing]
    aliases = {}
    if prior is not None:
        in_specs += [pl.BlockSpec(memory_space=pl.ANY)]
        aliases = {2 + len(operands): 0}
        operands += [prior]
    scratch, kernel, name = [], route_x_kernel, "route_x"
    if sizes is not None:
        scratch = [pltpu.VMEM((dps * PREF_DP, sizes[0], features), F32)]
        kernel, name = route_g_kernel, "route_g"
    return pl.pallas_call(
        functools.partial(kernel, (dps, cap, *(sizes or ()))),
        out_shape=(
            jax.ShapeDtypeStruct((dps, cap, n_e * features), BF16),
            jax.ShapeDtypeStruct((dps, cap, features), BF16),
        ),
        grid_spec=pltpu.PrefetchScalarGridSpec(
            num_scalar_prefetch=2,
            grid=(1,),
            in_specs=in_specs,
            out_specs=(block, pl.BlockSpec((dps, cap, features), lambda i, my, pid: (0, 0, 0))),
            scratch_shapes=scratch,
        ),
        input_output_aliases=aliases,
        compiler_params=pltpu.CompilerParams(vmem_limit_bytes=56 * MIB),
        cost_estimate=pl.CostEstimate(flops=4 * GFLOP // 2, bytes_accessed=16 * MIB, transcendentals=0),
        name=name,
    )(scalars, prefix_ids, *operands)


def routed_rows(pieces, my_dp, my_e, prefix_ids, routing, sizes):
    whole, away = None, []
    n_e, features = lax.axis_size("expert"), pieces[0, 0][0].shape[-1]
    for k in range(n_e // 4):
        for y in range(2):
            whole, part = route(pieces, y, k, my_dp, my_e, prefix_ids, routing, whole, sizes)
            away.append((2 * y + 4 * k, send(part, C)))
    for me, part in away:
        whole = lax.dynamic_update_slice(whole, part, (0, 0, (my_e ^ me ^ 1) * features))
    return whole.reshape(-1, n_e * features)


def dx_kernel(my_ref, da, db, dl, gate_w, up_w, router, tokens_of, out):
    nt = (((1,), (1,)), ((), ()))
    total = lax.dot_general(da[...], gate_w[...], nt, preferred_element_type=F32)
    total = total + lax.dot_general(db[...], up_w[...], nt, preferred_element_type=F32)
    total = total + jnp.dot(dl[...], router[0], preferred_element_type=F32)
    fours, tok, cap = tokens_of.shape
    for four in range(fours):
        place = (my_ref[1] // 4) ^ four
        rows = total[four * cap : (four + 1) * cap].astype(BF16)
        by_token = jnp.dot(tokens_of[place], rows, preferred_element_type=F32)
        out[0, pl.ds(pl.multiple_of(place * tok, tok), tok)] = by_token.astype(BF16)


def dx_tokens(d_a, d_b, dl, gate_w, up_w, routers, tokens_of, my_dp, my_e, top):
    rows, hidden = d_a.shape
    features = routers.shape[2]
    all_tok = tokens_of.shape[0] * tokens_of.shape[1]
    cuts = 2 if features % 256 == 0 else 1
    wide = features // cuts
    full = lambda *shape: pl.BlockSpec(shape, lambda i, j, my: (0,) * len(shape))
    weight = pl.BlockSpec((wide, hidden), lambda i, j, my: ((my[0] ^ (top - i)) * cuts + j, 0))
    return pl.pallas_call(
        dx_kernel,
        out_shape=jax.ShapeDtypeStruct((2, all_tok, features), BF16),
        grid_spec=pltpu.PrefetchScalarGridSpec(
            num_scalar_prefetch=1,
            grid=(2, cuts),
            in_specs=[
                full(rows, hidden),
                full(rows, hidden),
                full(*dl.shape),
                weight,
                weight,
                pl.BlockSpec((1, routers.shape[1], wide), lambda i, j, my: (top - i, 0, j)),
                full(*tokens_of.shape),
            ],
            out_specs=pl.BlockSpec((1, all_tok, wide), lambda i, j, my: (i, 0, j)),
        ),
        compiler_params=pltpu.CompilerParams(vmem_limit_bytes=56 * MIB),
        cost_estimate=pl.CostEstimate(flops=12 * GFLOP, bytes_accessed=12 * MIB, transcendentals=0),
        name="dx",
    )(jnp.stack([my_e, my_dp]).astype(jnp.int32), d_a, d_b, dl, gate_w, up_w, routers, tokens_of)


def add(*terms):
    total = terms[0].astype(F32)
    for term in terms[1:]:
        total = total + term.astype(F32)
    return total.astype(BF16)


def reduce_tokens(parts):
    n_e, n_dp = lax.axis_size("expert"), lax.axis_size("dp")
    for bit in reversed(bits(n_e, 2)):
        for me in range(bit):
            parts[me] = add(parts[me], send(parts.pop(me + bit), (0, bit)))
    for bit in reversed(bits(n_dp, 3)):
        for me in parts:
            parts[me] = add(parts[me][:bit], send(parts[me][bit:], (bit, 0)))
    _, tok, features = parts[0].shape
    half = tok // 2
    near, far = {}, {}
    for me in (2, 0):
        mine = parts[me].reshape(4, 2, tok, features)
        other = send(parts[me + 1], C).reshape(4, 2, tok, features)
        for x in range(2):
            near[me, x] = add(mine[:, x, :half], other[:, x, :half])
            if me == 0:
                far[me, x] = add(mine[:, x, half:], other[:, x, half:])
        if me == 2:
            far_y = add(mine[:, :, half:], other[:, :, half:])
    from_y = send(far_y, Y)
    near_y = add(near[2, 0], send(near[2, 1], X))
    far_1 = add(far[0, 1], from_y[:, 1])
    far_0 = add(far[0, 0], from_y[:, 0])
    near_0 = add(near[0, 0], send(near[0, 1], X))
    a = add(near_0, send(near_y, Y))
    b = add(far_0, send(far_1, X))
    both = [jnp.concatenate([a[z], b[z]], axis=0) for z in range(4)]
    both[2] = add(both[2], send(both[3], Z1))
    return add(both[0], send(both[2], Z2), send(both[1], Z1))


def body(
    tokens,
    suffix_cotangent,
    prefix_partials,
    prefix_of_seq,
    expert_ids,
    router_weight,
    gate_weight,
    up_weight,
    down_weight,
    gate_pre,
    up_pre,
):
    n_dp, n_e = lax.axis_size("dp"), lax.axis_size("expert")
    my_dp, my_e = lax.axis_index("dp"), lax.axis_index("expert")
    tok, features = tokens.shape
    seqs, pblk, _ = prefix_partials.shape
    suf = suffix_cotangent.shape[0]
    experts = router_weight.shape[1]
    row_total, hidden_here = gate_pre.shape[1:]
    cap = row_total // n_dp

    raw = jnp.concatenate([suffix_cotangent, prefix_partials.reshape(seqs * pblk, features)], axis=0)
    router_t = router_weight.T
    logits_here = lax.dot_general(router_t, tokens, (((1,), (1,)), ((), ())), preferred_element_type=F32)
    seq_row = jnp.pad(prefix_of_seq.astype(F32)[None], ((0, 0), (0, tok - seqs)))
    rest = jnp.concatenate([expert_ids.T.astype(F32), seq_row], axis=0)
    small = SmallGather(logits_here, router_t.astype(F32), rest)
    small.step()
    pieces = gather_tree(raw)
    for mask in SMALL_AT:
        small.step(pieces[mask])
    column = gather_column(tokens, pieces[X_AT])
    small, routers = small.finish()

    small = jnp.take(small, my_dp ^ jnp.arange(n_dp, dtype=jnp.int32), axis=0)
    logits = small[:, :experts]
    ids = small[:, experts : experts + 2].astype(jnp.int32)
    prefix_ids = small[:, experts + 2, :seqs].astype(jnp.int32).reshape(-1)
    first, second = ids[:, 0], ids[:, 1]
    iota_e = jnp.arange(experts, dtype=jnp.int32)[None, :, None]
    is_first = (first[:, None] == iota_e).astype(F32)
    is_second = (second[:, None] == iota_e).astype(F32)
    first_prob = jax.nn.sigmoid(jnp.sum(logits * (is_first - is_second), axis=1))
    second_prob = 1.0 - first_prob
    earlier = jnp.triu(jnp.ones((tok, tok), F32), 1)
    slots = jnp.arange(cap, dtype=jnp.int32)[None, :, None]

    def placing(expert):
        mine = (first == expert) | (second == expert)
        slot = jnp.dot(mine.astype(F32), earlier).astype(jnp.int32)
        slot = jnp.where(mine, slot, -1)
        return slot, slot[:, None, :] == slots

    slot, placed = placing(my_e)
    _, placed_other = placing(my_e ^ 1)
    routing = jnp.concatenate([placed, placed_other], axis=1).astype(BF16)
    relative = my_dp ^ jnp.arange(n_dp, dtype=jnp.int32)
    row_of = jnp.where(slot < 0, -1, slot + cap * (jnp.arange(n_dp, dtype=jnp.int32) % 4)[:, None])
    row_of = jnp.take(row_of, relative, axis=0).reshape(-1, 4 * tok, 1)
    tokens_of = (row_of == jnp.arange(4 * cap, dtype=jnp.int32)[None, None]).astype(BF16)
    prob_here = jnp.where(first == my_e, first_prob, second_prob)
    weight_col = (
        jnp.sum(jnp.where(placed, prob_here[:, None, :], 0.0), axis=2)
        .astype(BF16)
        .astype(F32)
        .reshape(row_total, 1)
    )
    other = jnp.where(first == my_e, second, first)
    product = first_prob * second_prob
    router_col = jnp.stack(
        [
            jnp.sum(
                jnp.where(
                    placed,
                    (
                        product
                        * ((my_e == e).astype(F32) - (other == e).astype(F32))
                    )[:, None, :],
                    0.0,
                ),
                axis=2,
            ).reshape(row_total)
            for e in range(experts)
        ],
        axis=1,
    )

    g_pieces = {(md, y): (pieces[md, 2 * y][None], 0) for md in range(8) for y in range(2)}
    rows_g = routed_rows(g_pieces, my_dp, my_e, prefix_ids, routing, (pblk, seqs, suf))
    over_x, over_y = send(column, X), send(column, Y)

    gate_w, up_w, down_w = gate_weight[0], up_weight[0], down_weight[0]
    gate_act = gate_pre[0].astype(F32)
    up_act = up_pre[0].astype(F32)
    sigmoid_a = jax.nn.sigmoid(gate_act)
    activation = gate_act * sigmoid_a
    slope = sigmoid_a * (1.0 + gate_act * (1.0 - sigmoid_a))
    hidden = activation * up_act
    d_hidden = lax.dot_general(
        rows_g, down_w, (((1,), (1,)), ((), ())), preferred_element_type=F32
    )
    dots = jnp.sum(hidden * d_hidden, axis=1)
    scaled = weight_col * d_hidden
    weighted = (weight_col * hidden).astype(BF16)
    d_a = (scaled * up_act * slope).astype(BF16)
    d_b = (scaled * activation).astype(BF16)

    d_a, d_b, over_x, over_y = lax.optimization_barrier((d_a, d_b, over_x, over_y))
    corner = send(over_y[:2], X), send(over_x[2:], Y)
    dl = dots[:, None] * router_col
    dl_high = dl.astype(BF16)
    dl_low = (dl - dl_high.astype(F32)).astype(BF16)
    dl = jnp.concatenate([dl_high, dl_low], axis=1)
    routers = jnp.concatenate([routers, routers], axis=1).astype(BF16)
    parts = {}
    for top in range(n_e - 1, 0, -2):
        if top == 1:
            d_a, d_b, corner = lax.optimization_barrier((d_a, d_b, corner))
        pair = dx_tokens(d_a, d_b, dl, gate_w, up_w, routers, tokens_of, my_dp, my_e, top)
        for i in range(2):
            parts[top - i] = pair[i].reshape(n_dp, tok, features)
    x_pieces = {}
    for z in range(4):
        x_pieces[2 * z, 0], x_pieces[2 * z + 1, 0] = (column, z), (over_x, z)
        x_pieces[2 * z, 1], x_pieces[2 * z + 1, 1] = (over_y, z), (corner[z // 2], z % 2)
    rows_x = routed_rows(x_pieces, my_dp, my_e, prefix_ids, routing, None)
    d_tokens = reduce_tokens(parts)

    tn = (((0,), (0,)), ((), ()))
    grad_down = lax.dot_general(weighted, rows_g, tn, preferred_element_type=F32)
    grad_gate = lax.dot_general(rows_x, d_a, tn, preferred_element_type=F32)
    grad_up = lax.dot_general(rows_x, d_b, tn, preferred_element_type=F32)
    return (
        d_tokens,
        grad_gate.astype(BF16)[None],
        grad_up.astype(BF16)[None],
        grad_down.astype(BF16)[None],
    )


def solution(mesh):
    return jax.shard_map(
        body,
        mesh=mesh,
        in_specs=(
            P("dp", "expert"),
            P("dp", "expert"),
            P("dp", None, "expert"),
            P("dp"),
            P("dp", None),
            P("expert", None),
            P("expert", None, "dp"),
            P("expert", None, "dp"),
            P("expert", "dp", None),
            P("expert", None, "dp"),
            P("expert", None, "dp"),
        ),
        out_specs=(
            P("dp", "expert"),
            P("expert", None, "dp"),
            P("expert", None, "dp"),
            P("expert", "dp", None),
        ),
        check_vma=False,
    )
```

time: 383 us -> 187 us (0.49)
  waiting for transfers between devices: 187 us -> 21.8 us
  blocking collectives: 65.5 us -> 0 us
  starting transfers between devices: 6.85 us -> 52.6 us
  Pallas kernels: 0 us -> 45.2 us
  matrix products: 60.2 us -> 35.7 us
  between operations: 16.1 us -> 1.12 us
  local copies, waits for them, and re-layouts: 21.1 us -> 13.1 us
  other arithmetic: 24.6 us -> 16.6 us
    unnamed x5 -> x0, waiting for transfers between devices: 73.4 us -> none
    reduce_scatter x1 -> x0, waiting for transfers between devices: 62.2 us -> none  [body(): lax.psum_scatter(dx_rows.astype(jnp.bfloat16), 'dp', scatter_dimension=0,...]
    ppermute x0 -> x41, starting transfers between devices: none -> 52.6 us  [send(): return lax.ppermute(value, AXES, pairs)]
    all_gather x2 -> x0, waiting for transfers between devices: 49 us -> none  [the longest x1 49 us: body(): piece_g = lax.all_gather(rows_g[0], 'dp', axis=0, tiled=True)]
    pallas_call x0 -> x6, Pallas kernels: none -> 45.2 us  [the longest x2 27.4 us: dx_tokens(): pl.pallas_call(dx_kernel, out_shape=jax.ShapeDtypeStruct((2, all_tok, fea...]
    unnamed x2 -> x0, blocking collectives: 37.5 us -> none
    dot_general x11 -> x7, matrix products: 60.2 us -> 35.7 us  [the longest x1 10.7 us: body(): lax.dot_general(rows_g, down_w, (((1,), (1,)), ((), ())), preferred_eleme...]
    all_to_all x2 -> x0, blocking collectives: 21.9 us -> none  [the longest x1 11 us: body(): lax.all_to_all(send_g, 'expert', split_axis=0, concat_axis=2, tiled=True)]
  transfers between devices with their start and end apart: 6 -> 41, of which waited for: 4 -> 12; matrix products, arithmetic and copies ran while one was open for 18% -> 32% of each run, Pallas kernels for 0% -> 24%
where the time goes in v1:
time: 187 us; the launch traced here: 186 us
  starting transfers between devices  52.6 us (28%)
  Pallas kernels  45.2 us (24%)
  matrix products  35.7 us (19%)
  waiting for transfers between devices  21.8 us (12%)
  other arithmetic  16.6 us (9%)
  local copies, waits for them, and re-layouts  13.1 us (7%)
    ppermute x41, starting transfers between devices, send(): return lax.ppermute(value, AXES, pairs)  52.6 us
    pallas_call x2, Pallas kernels, dx_tokens(): pl.pallas_call(dx_kernel, out_shape=jax.ShapeDtypeStruct((2, all_tok, fea...  27.4 us
    ppermute x41, waiting for transfers between devices, send(): return lax.ppermute(value, AXES, pairs)  21.8 us
    pallas_call x4, Pallas kernels, route(): pl.pallas_call(functools.partial(kernel, (dps, cap, *(sizes or ()))), out...  17.8 us
    dot_general x1, matrix products, body(): lax.dot_general(rows_g, down_w, (((1,), (1,)), ((), ())), preferred_eleme...  10.7 us
    dot_general x1, matrix products, body(): lax.dot_general(weighted, rows_g, tn, preferred_element_type=F32)  9.55 us
    dot_general x1, matrix products, body(): grad_up = lax.dot_general(rows_x, d_b, tn, preferred_element_type=F32)  7.04 us
    dot_general x1, matrix products, body(): grad_gate = lax.dot_general(rows_x, d_a, tn, preferred_element_type=F32)  7.04 us
  transfers between devices with their start and end apart: 41, of which 12 were waited for; matrix products, arithmetic and copies ran while one was open for 32% of the time, Pallas kernels for 24%

profile of v1, /device:TPU:0, one launch (start us, length us, event | category | flops | bytes accessed | tf_op | source)
XLA Modules:
  0.0 186.1 jit_solution(5817983212246082530)
XLA Ops:
  0.6 1.8 fusion.37
  2.4 3.0 %collective-permute-start.1 = (bf16[1,1,192,768]{3,2,1,0:T(8,128)(2,1)S(1)}, bf16[1,1,192,768]{3,2,1,0:T(8,128)(2,1)S(1)}, u32[]{:S(2)}, u32[]{:S(2)}) collective-permute-start(bf16[1,1,192,768]{3,2,1,0:T(8,128)(2,1)S(1)} %get-tuple-element.71), channel_id=1, source_target_pairs={{0,8},{1,9},{2,10},{3,11},{4,12},{5,13},{6,14},{7,15},{8,0},{9,1},... | collective-permute-start | bytes 884744 | tf_op jit(solution)/shard_map/ppermute | solution.py:29
  5.4 2.6 %collective-permute-start.3 = (bf16[1,1,192,768]{3,2,1,0:T(8,128)(2,1)S(1)}, bf16[1,1,192,768]{3,2,1,0:T(8,128)(2,1)S(1)}, u32[]{:S(2)}, u32[]{:S(2)}) collective-permute-start(bf16[1,1,192,768]{3,2,1,0:T(8,128)(2,1)S(1)} %get-tuple-element.71), channel_id=1, source_target_pairs={{0,16},{1,17},{2,18},{3,19},{4,20},{5,21},{6,22},{7,23},{8,24},{9,... | collective-permute-start | bytes 884744 | tf_op jit(solution)/shard_map/ppermute | solution.py:29
  8.0 1.5 collective-permute-start.10
  9.6 1.5 collective-permute-start.11
  11.7 1.1 fusion.75
  15.0 3.6 %collective-permute-done.1 = bf16[1,1,192,768]{3,2,1,0:T(8,128)(2,1)S(1)} collective-permute-done((bf16[1,1,192,768]{3,2,1,0:T(8,128)(2,1)S(1)}, bf16[1,1,192,768]{3,2,1,0:T(8,128)(2,1)S(1)}, u32[]{:S(2)}, u32[]{:S(2)}) %collective-permute-start.1) | collective-permute-done | bytes 294944 | tf_op jit(solution)/shard_map/ppermute | solution.py:29
  18.7 1.7 collective-permute-start.2
  21.6 1.5 collective-permute-start.7
  23.2 1.6 collective-permute-start.4
  25.4 1.5 collective-permute-done.4
  26.9 1.5 collective-permute-start.16
  29.2 1.2 collective-permute-start.8
  30.4 0.9 collective-permute-start.6
  31.3 1.6 collective-permute-start.14
  32.9 1.5 collective-permute-start.12
  34.5 2.0 %collective-permute-done.6 = f32[2,8,128]{2,1,0:T(8,128)S(1)} collective-permute-done((f32[2,8,128]{2,1,0:T(8,128)S(1)}, f32[2,8,128]{2,1,0:T(8,128)S(1)}, u32[]{:S(2)}, u32[]{:S(2)}) %collective-permute-start.6) | collective-permute-done | bytes 8224 | tf_op jit(solution)/shard_map/ppermute | solution.py:29
  36.5 1.6 collective-permute-start.13
  38.1 1.6 collective-permute-start.9
  40.3 1.4 collective-permute-start.17
  41.7 1.1 collective-permute-done.9
  42.9 1.5 collective-permute-start.19
  45.5 0.8 add_convert_fusion.9.refs_8_
  46.3 3.0 %collective-permute-start.23 = (bf16[1,1,128,768]{3,2,1,0:T(8,128)(2,1)S(1)}, bf16[1,1,128,768]{3,2,1,0:T(8,128)(2,1)S(1)}, u32[]{:S(2)}, u32[]{:S(2)}) collective-permute-start(bf16[1,1,128,768]{3,2,1,0:T(8,128)(2,1)S(1)} %bitcast.220), channel_id=1, source_target_pairs={{0,16},{1,17},{2,18},{3,19},{4,20},{5,21},{6,22},{7,23},{8,24},{9,... | collective-permute-start | bytes 589832 | tf_op jit(solution)/shard_map/ppermute | solution.py:29
  49.4 1.1 collective-permute-start.15
  50.4 2.0 %collective-permute-start.18 = (bf16[1,1,192,768]{3,2,1,0:T(8,128)(2,1)}, bf16[1,1,192,768]{3,2,1,0:T(8,128)(2,1)}, u32[]{:S(2)}, u32[]{:S(2)}) collective-permute-start(bf16[1,1,192,768]{3,2,1,0:T(8,128)(2,1)} %collective-permute-done.17), channel_id=1, source_target_pairs={{0,8},{1,9},{2,10},{3,11},{4,12},{5,13},{6,14},{7,15},{8,0},{9,1},... | collective-permute-start | bytes 884744 | tf_op jit(solution)/shard_map/ppermute | solution.py:29
  53.1 4.7 %route_g.2 = (bf16[8,80,3072]{2,1,0:T(8,128)(2,1)}, bf16[8,80,768]{2,1,0:T(8,128)(2,1)}) custom-call(s32[2]{0:T(128)} %pad_add_fusion.2.my_ref, s32[32]{0:T(128)} %convert_element_type.338.pid_ref, bf16[1,1,1,192,768]{4,3,2,1,0:T(8,128)(2,1)} %get-tuple-element.70.refs_0_, bf16[1,1,1,192,768]{4,3,2,1,0:T(8,128)(2,1)} %bitcast.249, ...), custom_call_target="tpu_custom_call" | custom-call | flops 2000000000 | bytes 16777216 | tf_op jit(solution)/shard_map/route_g/pallas_call | solution.py:166
  57.9 2.0 %collective-permute-start.24 = (bf16[1,1,128,768]{3,2,1,0:T(8,128)(2,1)S(1)}, bf16[1,1,128,768]{3,2,1,0:T(8,128)(2,1)S(1)}, u32[]{:S(2)}, u32[]{:S(2)}) collective-permute-start(bf16[1,1,128,768]{3,2,1,0:T(8,128)(2,1)S(1)} %collective-permute-done.23), channel_id=1, source_target_pairs={{0,8},{1,9},{2,10},{3,11},{4,12},{5,13},{6,14},{7,15},{8,0},{9,1},... | collective-permute-start | bytes 589832 | tf_op jit(solution)/shard_map/ppermute | solution.py:29
  60.1 4.7 %route_g.3 = (bf16[8,80,3072]{2,1,0:T(8,128)(2,1)}, bf16[8,80,768]{2,1,0:T(8,128)(2,1)}) custom-call(s32[2]{0:T(128)} %pad_add_fusion.1.my_ref, s32[32]{0:T(128)} %convert_element_type.338.pid_ref, bf16[1,1,1,192,768]{4,3,2,1,0:T(8,128)(2,1)} %bitcast.246, bf16[1,1,1,192,768]{4,3,2,1,0:T(8,128)(2,1)} %bitcast.15.refs_1_, ...), custom_call_target="tpu_custom_call", output_to_operand_aliasing={{0}: (11, {})} | custom-call | flops 2000000000 | bytes 16777216 | tf_op jit(solution)/shard_map/route_g/pallas_call | solution.py:166
  68.1 1.1 fusion.21.tokens_of
  69.4 2.7 %collective-permute-start.25 = (bf16[4,1,1,128,768]{4,3,2,1,0:T(8,128)(2,1)S(1)}, bf16[4,1,1,128,768]{4,3,2,1,0:T(8,128)(2,1)S(1)}, u32[]{:S(2)}, u32[]{:S(2)}) collective-permute-start(bf16[4,1,1,128,768]{4,3,2,1,0:T(8,128)(2,1)S(1)} %pad_maximum_fusion.refs_0_.refs_2_.refs_4_.refs_6_), channel_id=1, source_target_pairs={{0,4},{1,5},{2,6},{3,7},{4,0},{5,1},{6,2},{7,3},{8,12},{9,13},{10,... | collective-permute-start | bytes 2359304 | tf_op jit(solution)/shard_map/ppermute | solution.py:29
  72.1 1.3 collective-permute-start.26
  73.4 1.0 constant_dynamic-update-slice_fusion.3
  74.4 1.0 constant_dynamic-update-slice_fusion.2
  75.4 10.7 %fusion.10 = (f32[640]{0:T(1024)S(1)}, bf16[640,1024]{1,0:T(8,128)(2,1)}, bf16[640,1024]{1,0:T(8,128)(2,1)}) fusion(bf16[1,640,1024]{2,1,0:T(8,128)(2,1)S(1)} %copy-done.11, bf16[1,640,1024]{2,1,0:T(8,128)(2,1)S(1)} %copy-done.12, f32[640]{0:T(1024)S(1)} %copy-done.8, bf16[640,3072]{1,0:T(8,128)(2,1)} %bitcast.244, bf16[1,1024,3072]{2,1,0:T(8,128)(2,1)} %param.19), kind=kOutput, calls=%fused_computation.20 | convolution fusion | flops 4038983168 | bytes 15471616 | tf_op jit(solution)/shard_map/dot_general | solution.py:380
  86.1 4.1 %collective-permute-done.25.refs_1_.refs_3_.refs_5_.refs_7_ = bf16[4,1,1,128,768]{4,3,2,1,0:T(8,128)(2,1)S(1)} collective-permute-done((bf16[4,1,1,128,768]{4,3,2,1,0:T(8,128)(2,1)S(1)}, bf16[4,1,1,128,768]{4,3,2,1,0:T(8,128)(2,1)S(1)}, u32[]{:S(2)}, u32[]{:S(2)}) %collective-permute-start.25) | collective-permute-done | bytes 786464 | tf_op jit(solution)/shard_map/ppermute | solution.py:29
  90.3 1.5 collective-permute-done.26.refs_0_.refs_2_.refs_4_.refs_6_
  91.8 0.9 copy.41.dl
  92.7 1.3 collective-permute-start.27
  94.0 1.0 slice.126
  95.0 1.4 collective-permute-start.28
  96.4 13.8 %dx.3 = bf16[2,1024,768]{2,1,0:T(8,128)(2,1)} custom-call(s32[2]{0:T(128)} %pad_add_fusion.my_ref, bf16[640,1024]{1,0:T(8,128)(2,1)} %get-tuple-element.38.da, bf16[640,1024]{1,0:T(8,128)(2,1)} %get-tuple-element.39.db, bf16[640,8]{1,0:T(8,128)(2,1)} %copy.41.dl, bf16[3072,1024]{1,0:T(8,128)(2,1)} %bitcast.240, bf16[3072,1024]{1,0:T(8,128)(2,1)} %bitcast.242, ...), custom_call_target="tpu_custom_call" | custom-call | flops 12000000000 | bytes 12582912 | tf_op jit(solution)/shard_map/dx/pallas_call | solution.py:219
  110.2 3.2 %fusion.73 = (bf16[1,1024,768]{2,1,0:T(8,128)(2,1)S(1)}, bf16[1,1024,768]{2,1,0:T(8,128)(2,1)}) fusion(bf16[2,1024,768]{2,1,0:T(8,128)(2,1)} %dx.3), kind=kLoop, calls=%fused_computation.185 | loop fusion | bytes 6291456 | tf_op jit(solution)/shard_map/slice | solution.py:402
  113.4 13.6 %dx.2 = bf16[2,1024,768]{2,1,0:T(8,128)(2,1)} custom-call(s32[2]{0:T(128)} %pad_add_fusion.my_ref, bf16[640,1024]{1,0:T(8,128)(2,1)} %get-tuple-element.38.da, bf16[640,1024]{1,0:T(8,128)(2,1)} %get-tuple-element.39.db, bf16[640,8]{1,0:T(8,128)(2,1)} %copy.41.dl, bf16[3072,1024]{1,0:T(8,128)(2,1)} %bitcast.241, bf16[3072,1024]{1,0:T(8,128)(2,1)} %bitcast.243, ...), custom_call_target="tpu_custom_call" | custom-call | flops 12000000000 | bytes 12582912 | tf_op jit(solution)/shard_map/dx/pallas_call | solution.py:219
  127.1 2.1 %fusion.72 = (bf16[1,1024,768]{2,1,0:T(8,128)(2,1)S(1)}, bf16[1,1024,768]{2,1,0:T(8,128)(2,1)S(1)}) fusion(bf16[2,1024,768]{2,1,0:T(8,128)(2,1)} %dx.2), kind=kLoop, calls=%fused_computation.184 | loop fusion | bytes 6291456 | tf_op jit(solution)/shard_map/slice | solution.py:402
  129.7 0.8 fusion.34
  130.6 0.8 collective-permute-start.32
  131.6 0.8 collective-permute-start.34
  132.3 4.1 %route_x.2 = (bf16[8,80,3072]{2,1,0:T(8,128)(2,1)}, bf16[8,80,768]{2,1,0:T(8,128)(2,1)}) custom-call(s32[2]{0:T(128)} %pad_add_fusion.2.my_ref, s32[32]{0:T(128)} %convert_element_type.338.pid_ref, bf16[4,1,1,128,768]{4,3,2,1,0:T(8,128)(2,1)} %copy-done.5, bf16[4,1,1,128,768]{4,3,2,1,0:T(8,128)(2,1)} %copy-done.6, bf16[4,1,1,128,768]{4,3,2,1,0:T(8,128)(2,1)} %copy-done.5, ...), custom_call_target="tpu_custom_call" | custom-call | flops 2000000000 | bytes 16777216 | tf_op jit(solution)/shard_map/route_x/pallas_call | solution.py:166
  136.5 4.2 %route_x.3 = (bf16[8,80,3072]{2,1,0:T(8,128)(2,1)}, bf16[8,80,768]{2,1,0:T(8,128)(2,1)}) custom-call(s32[2]{0:T(128)} %pad_add_fusion.1.my_ref, s32[32]{0:T(128)} %convert_element_type.338.pid_ref, bf16[4,1,1,128,768]{4,3,2,1,0:T(8,128)(2,1)} %copy-done, bf16[2,1,1,128,768]{4,3,2,1,0:T(8,128)(2,1)} %copy-done.2, ...), custom_call_target="tpu_custom_call", output_to_operand_aliasing={{0}: (11, {})} | custom-call | flops 2000000000 | bytes 16777216 | tf_op jit(solution)/shard_map/route_x/pallas_call | solution.py:166
  141.9 1.1 fusion.29
  143.1 1.1 collective-permute-start.33
  144.2 1.1 fusion.32
  145.3 1.1 collective-permute-start.30
  146.4 5.8 %collective-permute-done.34 = bf16[4,2,64,768]{3,2,0,1:T(8,128)(2,1)} collective-permute-done((bf16[4,2,64,768]{3,2,0,1:T(8,128)(2,1)S(1)}, bf16[4,2,64,768]{3,2,0,1:T(8,128)(2,1)}, u32[]{:S(2)}, u32[]{:S(2)}) %collective-permute-start.34) | collective-permute-done | bytes 786464 | tf_op jit(solution)/shard_map/ppermute | solution.py:29
  152.2 1.3 fusion.36
  153.4 1.3 collective-permute-start.35
  154.7 9.6 %convert_bitcast_fusion = bf16[1,1024,3072]{2,1,0:T(8,128)(2,1)} fusion(bf16[640,3072]{1,0:T(8,128)(2,1)S(1)} %bitcast.245, bf16[1,640,1024]{2,1,0:T(8,128)(2,1)} %param.21, bf16[1,640,1024]{2,1,0:T(8,128)(2,1)} %param.20, f32[640]{0:T(1024)S(1)} %copy-done.9), kind=kOutput, calls=%fused_computation.4 | convolution fusion | flops 4035575808 | bytes 12847616 | tf_op jit(solution)/shard_map/dot_general | solution.py:411
  164.6 1.7 add_convert_fusion.4
  166.4 1.1 collective-permute-start.36
  167.6 7.0 %convert_bitcast_fusion.2 = bf16[1,3072,1024]{2,1,0:T(8,128)(2,1)} fusion(bf16[640,3072]{1,0:T(8,128)(2,1)S(1)} %bitcast.214, bf16[640,1024]{1,0:T(8,128)(2,1)S(1)} %copy-done.22), kind=kOutput, calls=%fused_computation.6 | convolution fusion | flops 4029677568 | bytes 11534336 | tf_op jit(solution)/shard_map/dot_general | solution.py:412
  174.6 1.0 collective-permute-start.38
  175.7 2.3 %collective-permute-start.37 = (bf16[128,768]{1,0:T(8,128)(2,1)S(1)}, bf16[128,768]{1,0:T(8,128)(2,1)S(1)}, u32[]{:S(2)}, u32[]{:S(2)}) collective-permute-start(bf16[128,768]{1,0:T(8,128)(2,1)S(1)} %add_convert_fusion.11), channel_id=1, source_target_pairs={{0,16},{1,17},{2,18},{3,19},{4,20},{5,21},{6,22},{7,23},{8,24},{9,... | collective-permute-start | bytes 589832 | tf_op jit(solution)/shard_map/ppermute | solution.py:29
  178.0 7.0 %convert_bitcast_fusion.1 = bf16[1,3072,1024]{2,1,0:T(8,128)(2,1)} fusion(bf16[640,3072]{1,0:T(8,128)(2,1)S(1)} %bitcast.215, bf16[640,1024]{1,0:T(8,128)(2,1)S(1)} %copy-done.21), kind=kOutput, calls=%fused_computation.5 | convolution fusion | flops 4029677568 | bytes 11534336 | tf_op jit(solution)/shard_map/dot_general | solution.py:413
  (150 shorter events, 15.2 us)
Async XLA Ops:
  0.6 45.7 %copy-start.4 = (bf16[128,768]{1,0:T(8,128)(2,1)S(1)}, bf16[128,768]{1,0:T(8,128)(2,1)}, u32[]{:S(2)}) copy-start(bf16[128,768]{1,0:T(8,128)(2,1)} %param.11) | copy-start | bytes 589828
  2.4 16.2 %collective-permute-start.1 = (bf16[1,1,192,768]{3,2,1,0:T(8,128)(2,1)S(1)}, bf16[1,1,192,768]{3,2,1,0:T(8,128)(2,1)S(1)}, u32[]{:S(2)}, u32[]{:S(2)}) collective-permute-start(bf16[1,1,192,768]{3,2,1,0:T(8,128)(2,1)S(1)} %get-tuple-element.71), channel_id=1, source_target_pairs={{0,8},{1,9},{2,10},{3,11},{4,12},{5,13},{6,14},{7,15},{8,0},{9,1},... | collective-permute-start | bytes 884744 | tf_op jit(solution)/shard_map/ppermute | solution.py:29
  5.4 15.7 %collective-permute-start.3 = (bf16[1,1,192,768]{3,2,1,0:T(8,128)(2,1)S(1)}, bf16[1,1,192,768]{3,2,1,0:T(8,128)(2,1)S(1)}, u32[]{:S(2)}, u32[]{:S(2)}) collective-permute-start(bf16[1,1,192,768]{3,2,1,0:T(8,128)(2,1)S(1)} %get-tuple-element.71), channel_id=1, source_target_pairs={{0,16},{1,17},{2,18},{3,19},{4,20},{5,21},{6,22},{7,23},{8,24},{9,... | collective-permute-start | bytes 884744 | tf_op jit(solution)/shard_map/ppermute | solution.py:29
  8.0 23.3 %collective-permute-start.10 = (bf16[1,1,192,768]{3,2,1,0:T(8,128)(2,1)S(1)}, bf16[1,1,192,768]{3,2,1,0:T(8,128)(2,1)S(1)}, u32[]{:S(2)}, u32[]{:S(2)}) collective-permute-start(bf16[1,1,192,768]{3,2,1,0:T(8,128)(2,1)S(1)} %get-tuple-element.71), channel_id=1, source_target_pairs={{0,2},{1,3},{2,0},{3,1},{4,6},{5,7},{6,4},{7,5},{8,10},{9,11},{10,... | collective-permute-start | bytes 884744 | tf_op jit(solution)/shard_map/ppermute | solution.py:29
  9.6 23.4 %collective-permute-start.11 = (bf16[1,1,192,768]{3,2,1,0:T(8,128)(2,1)S(1)}, bf16[1,1,192,768]{3,2,1,0:T(8,128)(2,1)S(1)}, u32[]{:S(2)}, u32[]{:S(2)}) collective-permute-start(bf16[1,1,192,768]{3,2,1,0:T(8,128)(2,1)S(1)} %get-tuple-element.71), channel_id=1, source_target_pairs={{0,4},{1,5},{2,6},{3,7},{4,0},{5,1},{6,2},{7,3},{8,12},{9,13},{10,... | collective-permute-start | bytes 884744 | tf_op jit(solution)/shard_map/ppermute | solution.py:29
  12.9 2.1 %collective-permute-start = (f32[8,768]{1,0:T(8,128)S(1)}, f32[8,768]{1,0:T(8,128)S(1)}, u32[]{:S(2)}, u32[]{:S(2)}) collective-permute-start(f32[8,768]{1,0:T(8,128)S(1)} %select_maximum_fusion.1), channel_id=1, source_target_pairs={{0,1},{1,0},{2,3},{3,2},{4,5},{5,4},{6,7},{7,6},{8,9},{9,8},{10,11... | collective-permute-start | bytes 73736 | tf_op jit(solution)/shard_map/ppermute | solution.py:29
  18.7 34.5 %copy-start.14 = (bf16[1,1,192,768]{3,2,1,0:T(8,128)(2,1)}, bf16[1,1,192,768]{3,2,1,0:T(8,128)(2,1)S(1)}, u32[]{:S(2)}) copy-start(bf16[1,1,192,768]{3,2,1,0:T(8,128)(2,1)S(1)} %collective-permute-done.1) | copy-start | bytes 884740
  18.7 4.5 %collective-permute-start.2 = (f32[12,768]{1,0:T(8,128)S(1)}, f32[12,768]{1,0:T(8,128)S(1)}, u32[]{:S(2)}, u32[]{:S(2)}) collective-permute-start(f32[12,768]{1,0:T(8,128)S(1)} %fusion.41), channel_id=1, source_target_pairs={{0,2},{1,3},{2,0},{3,1},{4,6},{5,7},{6,4},{7,5},{8,10},{9,11},{10,... | collective-permute-start | bytes 110600 | tf_op jit(solution)/shard_map/ppermute | solution.py:29
  21.2 31.9 %copy-start.15 = (bf16[1,1,192,768]{3,2,1,0:T(8,128)(2,1)}, bf16[1,1,192,768]{3,2,1,0:T(8,128)(2,1)S(1)}, u32[]{:S(2)}) copy-start(bf16[1,1,192,768]{3,2,1,0:T(8,128)(2,1)S(1)} %collective-permute-done.3) | copy-start | bytes 884740
  21.2 9.2 %collective-permute-start.5 = (bf16[1,1,192,768]{3,2,1,0:T(8,128)(2,1)S(1)}, bf16[1,1,192,768]{3,2,1,0:T(8,128)(2,1)S(1)}, u32[]{:S(2)}, u32[]{:S(2)}) collective-permute-start(bf16[1,1,192,768]{3,2,1,0:T(8,128)(2,1)S(1)} %collective-permute-done.3), channel_id=1, source_target_pairs={{0,8},{1,9},{2,10},{3,11},{4,12},{5,13},{6,14},{7,15},{8,0},{9,1},... | collective-permute-start | bytes 884744 | tf_op jit(solution)/shard_map/ppermute | solution.py:29
  21.6 7.5 %collective-permute-start.7 = (bf16[1,1,192,768]{3,2,1,0:T(8,128)(2,1)S(1)}, bf16[1,1,192,768]{3,2,1,0:T(8,128)(2,1)S(1)}, u32[]{:S(2)}, u32[]{:S(2)}) collective-permute-start(bf16[1,1,192,768]{3,2,1,0:T(8,128)(2,1)S(1)} %collective-permute-done.3), channel_id=1, source_target_pairs={{0,2},{1,3},{2,0},{3,1},{4,6},{5,7},{6,4},{7,5},{8,10},{9,11},{10,... | collective-permute-start | bytes 884744 | tf_op jit(solution)/shard_map/ppermute | solution.py:29
  23.2 3.7 %collective-permute-start.4 = (f32[1,8,128]{2,1,0:T(8,128)S(1)}, f32[1,8,128]{2,1,0:T(8,128)S(1)}, u32[]{:S(2)}, u32[]{:S(2)}) collective-permute-start(f32[1,8,128]{2,1,0:T(8,128)S(1)} %pad_bitcast_fusion), channel_id=1, source_target_pairs={{0,4},{1,5},{2,6},{3,7},{4,0},{5,1},{6,2},{7,3},{8,12},{9,13},{10,... | collective-permute-start | bytes 12296 | tf_op jit(solution)/shard_map/ppermute | solution.py:29
  26.9 13.4 %collective-permute-start.16 = (bf16[1,1,192,768]{3,2,1,0:T(8,128)(2,1)S(1)}, bf16[1,1,192,768]{3,2,1,0:T(8,128)(2,1)S(1)}, u32[]{:S(2)}, u32[]{:S(2)}) collective-permute-start(bf16[1,1,192,768]{3,2,1,0:T(8,128)(2,1)S(1)} %collective-permute-done.3), channel_id=1, source_target_pairs={{0,4},{1,5},{2,6},{3,7},{4,0},{5,1},{6,2},{7,3},{8,12},{9,13},{10,... | collective-permute-start | bytes 884744 | tf_op jit(solution)/shard_map/ppermute | solution.py:29
  29.2 31.0 %copy-start.17 = (bf16[1,1,192,768]{3,2,1,0:T(8,128)(2,1)}, bf16[1,1,192,768]{3,2,1,0:T(8,128)(2,1)S(1)}, u32[]{:S(2)}) copy-start(bf16[1,1,192,768]{3,2,1,0:T(8,128)(2,1)S(1)} %collective-permute-done.7) | copy-start | bytes 884740
  29.2 8.9 %collective-permute-start.8 = (bf16[1,1,192,768]{3,2,1,0:T(8,128)(2,1)S(1)}, bf16[1,1,192,768]{3,2,1,0:T(8,128)(2,1)S(1)}, u32[]{:S(2)}, u32[]{:S(2)}) collective-permute-start(bf16[1,1,192,768]{3,2,1,0:T(8,128)(2,1)S(1)} %collective-permute-done.7), channel_id=1, source_target_pairs={{0,8},{1,9},{2,10},{3,11},{4,12},{5,13},{6,14},{7,15},{8,0},{9,1},... | collective-permute-start | bytes 884744 | tf_op jit(solution)/shard_map/ppermute | solution.py:29
  30.4 22.8 %copy-start.18 = (bf16[1,1,192,768]{3,2,1,0:T(8,128)(2,1)}, bf16[1,1,192,768]{3,2,1,0:T(8,128)(2,1)S(1)}, u32[]{:S(2)}) copy-start(bf16[1,1,192,768]{3,2,1,0:T(8,128)(2,1)S(1)} %collective-permute-done.5) | copy-start | bytes 884740
  30.4 6.1 %collective-permute-start.6 = (f32[2,8,128]{2,1,0:T(8,128)S(1)}, f32[2,8,128]{2,1,0:T(8,128)S(1)}, u32[]{:S(2)}, u32[]{:S(2)}) collective-permute-start(f32[2,8,128]{2,1,0:T(8,128)S(1)} %pad_maximum_fusion.8), channel_id=1, source_target_pairs={{0,8},{1,9},{2,10},{3,11},{4,12},{5,13},{6,14},{7,15},{8,0},{9,1},... | collective-permute-start | bytes 24584 | tf_op jit(solution)/shard_map/ppermute | solution.py:29
  31.3 26.5 %copy-start.13 = (bf16[1,1,192,768]{3,2,1,0:T(8,128)(2,1)}, bf16[1,1,192,768]{3,2,1,0:T(8,128)(2,1)S(1)}, u32[]{:S(2)}) copy-start(bf16[1,1,192,768]{3,2,1,0:T(8,128)(2,1)S(1)} %collective-permute-done.10) | copy-start | bytes 884740
  31.3 15.0 %collective-permute-start.14 = (bf16[1,1,192,768]{3,2,1,0:T(8,128)(2,1)S(1)}, bf16[1,1,192,768]{3,2,1,0:T(8,128)(2,1)}, u32[]{:S(2)}, u32[]{:S(2)}) collective-permute-start(bf16[1,1,192,768]{3,2,1,0:T(8,128)(2,1)S(1)} %collective-permute-done.1), channel_id=1, source_target_pairs={{0,4},{1,5},{2,6},{3,7},{4,0},{5,1},{6,2},{7,3},{8,12},{9,13},{10,... | collective-permute-start | bytes 884744 | tf_op jit(solution)/shard_map/ppermute | solution.py:29
  32.9 20.2 %copy-start.16 = (bf16[1,1,192,768]{3,2,1,0:T(8,128)(2,1)}, bf16[1,1,192,768]{3,2,1,0:T(8,128)(2,1)S(1)}, u32[]{:S(2)}) copy-start(bf16[1,1,192,768]{3,2,1,0:T(8,128)(2,1)S(1)} %collective-permute-done.11) | copy-start | bytes 884740
  32.9 24.9 %collective-permute-start.12 = (bf16[1,1,192,768]{3,2,1,0:T(8,128)(2,1)S(1)}, bf16[1,1,192,768]{3,2,1,0:T(8,128)(2,1)}, u32[]{:S(2)}, u32[]{:S(2)}) collective-permute-start(bf16[1,1,192,768]{3,2,1,0:T(8,128)(2,1)S(1)} %collective-permute-done.11), channel_id=1, source_target_pairs={{0,2},{1,3},{2,0},{3,1},{4,6},{5,7},{6,4},{7,5},{8,10},{9,11},{10,... | collective-permute-start | bytes 884744 | tf_op jit(solution)/shard_map/ppermute | solution.py:29
  36.5 23.5 %collective-permute-start.13 = (bf16[1,1,192,768]{3,2,1,0:T(8,128)(2,1)S(1)}, bf16[1,1,192,768]{3,2,1,0:T(8,128)(2,1)}, u32[]{:S(2)}, u32[]{:S(2)}) collective-permute-start(bf16[1,1,192,768]{3,2,1,0:T(8,128)(2,1)S(1)} %collective-permute-done.10), channel_id=1, source_target_pairs={{0,8},{1,9},{2,10},{3,11},{4,12},{5,13},{6,14},{7,15},{8,0},{9,1},... | collective-permute-start | bytes 884744 | tf_op jit(solution)/shard_map/ppermute | solution.py:29
  38.1 19.8 %copy-start.19 = (bf16[1,1,192,768]{3,2,1,0:T(8,128)(2,1)}, bf16[1,1,192,768]{3,2,1,0:T(8,128)(2,1)S(1)}, u32[]{:S(2)}) copy-start(bf16[1,1,192,768]{3,2,1,0:T(8,128)(2,1)S(1)} %collective-permute-done.8) | copy-start | bytes 884740
  38.1 4.8 %collective-permute-start.9 = (f32[4,8,128]{2,1,0:T(8,128)S(1)}, f32[4,8,128]{2,1,0:T(8,128)S(1)}, u32[]{:S(2)}, u32[]{:S(2)}) collective-permute-start(f32[4,8,128]{2,1,0:T(8,128)S(1)} %pad_maximum_fusion.6), channel_id=1, source_target_pairs={{0,16},{1,17},{2,18},{3,19},{4,20},{5,21},{6,22},{7,23},{8,24},{9,... | collective-permute-start | bytes 49160 | tf_op jit(solution)/shard_map/ppermute | solution.py:29
  40.3 12.8 %copy-start.20 = (bf16[1,1,192,768]{3,2,1,0:T(8,128)(2,1)}, bf16[1,1,192,768]{3,2,1,0:T(8,128)(2,1)S(1)}, u32[]{:S(2)}) copy-start(bf16[1,1,192,768]{3,2,1,0:T(8,128)(2,1)S(1)} %collective-permute-done.16) | copy-start | bytes 884740
  40.3 9.0 %collective-permute-start.17 = (bf16[1,1,192,768]{3,2,1,0:T(8,128)(2,1)S(1)}, bf16[1,1,192,768]{3,2,1,0:T(8,128)(2,1)}, u32[]{:S(2)}, u32[]{:S(2)}) collective-permute-start(bf16[1,1,192,768]{3,2,1,0:T(8,128)(2,1)S(1)} %collective-permute-done.16), channel_id=1, source_target_pairs={{0,2},{1,3},{2,0},{3,1},{4,6},{5,7},{6,4},{7,5},{8,10},{9,11},{10,... | collective-permute-start | bytes 884744 | tf_op jit(solution)/shard_map/ppermute | solution.py:29
  42.9 7.6 %collective-permute-start.19 = (bf16[1,1,192,768]{3,2,1,0:T(8,128)(2,1)S(1)}, bf16[1,1,192,768]{3,2,1,0:T(8,128)(2,1)}, u32[]{:S(2)}, u32[]{:S(2)}) collective-permute-start(bf16[1,1,192,768]{3,2,1,0:T(8,128)(2,1)S(1)} %collective-permute-done.5), channel_id=1, source_target_pairs={{0,4},{1,5},{2,6},{3,7},{4,0},{5,1},{6,2},{7,3},{8,12},{9,13},{10,... | collective-permute-start | bytes 884744 | tf_op jit(solution)/shard_map/ppermute | solution.py:29
  46.3 11.6 %collective-permute-start.23 = (bf16[1,1,128,768]{3,2,1,0:T(8,128)(2,1)S(1)}, bf16[1,1,128,768]{3,2,1,0:T(8,128)(2,1)S(1)}, u32[]{:S(2)}, u32[]{:S(2)}) collective-permute-start(bf16[1,1,128,768]{3,2,1,0:T(8,128)(2,1)S(1)} %bitcast.220), channel_id=1, source_target_pairs={{0,16},{1,17},{2,18},{3,19},{4,20},{5,21},{6,22},{7,23},{8,24},{9,... | collective-permute-start | bytes 589832 | tf_op jit(solution)/shard_map/ppermute | solution.py:29
  49.4 10.6 %collective-permute-start.15 = (bf16[1,1,192,768]{3,2,1,0:T(8,128)(2,1)}, bf16[1,1,192,768]{3,2,1,0:T(8,128)(2,1)}, u32[]{:S(2)}, u32[]{:S(2)}) collective-permute-start(bf16[1,1,192,768]{3,2,1,0:T(8,128)(2,1)} %collective-permute-done.14), channel_id=1, source_target_pairs={{0,2},{1,3},{2,0},{3,1},{4,6},{5,7},{6,4},{7,5},{8,10},{9,11},{10,... | collective-permute-start | bytes 884744 | tf_op jit(solution)/shard_map/ppermute | solution.py:29
  50.4 9.7 %collective-permute-start.18 = (bf16[1,1,192,768]{3,2,1,0:T(8,128)(2,1)}, bf16[1,1,192,768]{3,2,1,0:T(8,128)(2,1)}, u32[]{:S(2)}, u32[]{:S(2)}) collective-permute-start(bf16[1,1,192,768]{3,2,1,0:T(8,128)(2,1)} %collective-permute-done.17), channel_id=1, source_target_pairs={{0,8},{1,9},{2,10},{3,11},{4,12},{5,13},{6,14},{7,15},{8,0},{9,1},... | collective-permute-start | bytes 884744 | tf_op jit(solution)/shard_map/ppermute | solution.py:29
  57.9 11.4 %collective-permute-start.22 = (bf16[1,1,128,768]{3,2,1,0:T(8,128)(2,1)S(1)}, bf16[1,1,128,768]{3,2,1,0:T(8,128)(2,1)S(1)}, u32[]{:S(2)}, u32[]{:S(2)}) collective-permute-start(bf16[1,1,128,768]{3,2,1,0:T(8,128)(2,1)S(1)} %bitcast.221), channel_id=1, source_target_pairs={{0,8},{1,9},{2,10},{3,11},{4,12},{5,13},{6,14},{7,15},{8,0},{9,1},... | collective-permute-start | bytes 589832 | tf_op jit(solution)/shard_map/ppermute | solution.py:29
  57.9 11.3 %collective-permute-start.24 = (bf16[1,1,128,768]{3,2,1,0:T(8,128)(2,1)S(1)}, bf16[1,1,128,768]{3,2,1,0:T(8,128)(2,1)S(1)}, u32[]{:S(2)}, u32[]{:S(2)}) collective-permute-start(bf16[1,1,128,768]{3,2,1,0:T(8,128)(2,1)S(1)} %collective-permute-done.23), channel_id=1, source_target_pairs={{0,8},{1,9},{2,10},{3,11},{4,12},{5,13},{6,14},{7,15},{8,0},{9,1},... | collective-permute-start | bytes 589832 | tf_op jit(solution)/shard_map/ppermute | solution.py:29
  60.0 13.4 %collective-permute-start.20 = (bf16[8,80,768]{2,1,0:T(8,128)(2,1)}, bf16[8,80,768]{2,1,0:T(8,128)(2,1)S(1)}, u32[]{:S(2)}, u32[]{:S(2)}) collective-permute-start(bf16[8,80,768]{2,1,0:T(8,128)(2,1)} %get-tuple-element.31), channel_id=1, source_target_pairs={{0,1},{1,0},{2,3},{3,2},{4,5},{5,4},{6,7},{7,6},{8,9},{9,8},{10,11... | collective-permute-start | bytes 2949128 | tf_op jit(solution)/shard_map/ppermute | solution.py:29
  64.8 9.6 %collective-permute-start.21 = (bf16[8,80,768]{2,1,0:T(8,128)(2,1)}, bf16[8,80,768]{2,1,0:T(8,128)(2,1)S(1)}, u32[]{:S(2)}, u32[]{:S(2)}) collective-permute-start(bf16[8,80,768]{2,1,0:T(8,128)(2,1)} %get-tuple-element.32), channel_id=1, source_target_pairs={{0,1},{1,0},{2,3},{3,2},{4,5},{5,4},{6,7},{7,6},{8,9},{9,8},{10,11... | collective-permute-start | bytes 2949128 | tf_op jit(solution)/shard_map/ppermute | solution.py:29
  69.2 6.2 %copy-start.8 = (f32[640]{0:T(1024)S(1)}, f32[640]{0:T(1024)}, u32[]{:S(2)}) copy-start(f32[640]{0:T(1024)} %reshape.180) | copy-start | bytes 7684
  69.2 6.2 %copy-start.11 = (bf16[1,640,1024]{2,1,0:T(8,128)(2,1)S(1)}, bf16[1,640,1024]{2,1,0:T(8,128)(2,1)}, u32[]{:S(2)}) copy-start(bf16[1,640,1024]{2,1,0:T(8,128)(2,1)} %param.21) | copy-start | bytes 3932164
  69.2 6.2 %copy-start.12 = (bf16[1,640,1024]{2,1,0:T(8,128)(2,1)S(1)}, bf16[1,640,1024]{2,1,0:T(8,128)(2,1)}, u32[]{:S(2)}) copy-start(bf16[1,640,1024]{2,1,0:T(8,128)(2,1)} %param.20) | copy-start | bytes 3932164
  69.4 16.8 %copy-start.5 = (bf16[4,1,1,128,768]{4,3,2,1,0:T(8,128)(2,1)}, bf16[4,1,1,128,768]{4,3,2,1,0:T(8,128)(2,1)S(1)}, u32[]{:S(2)}) copy-start(bf16[4,1,1,128,768]{4,3,2,1,0:T(8,128)(2,1)S(1)} %pad_maximum_fusion.refs_0_.refs_2_.refs_4_.refs_6_) | copy-start | bytes 2359300
  69.4 20.9 %collective-permute-start.25 = (bf16[4,1,1,128,768]{4,3,2,1,0:T(8,128)(2,1)S(1)}, bf16[4,1,1,128,768]{4,3,2,1,0:T(8,128)(2,1)S(1)}, u32[]{:S(2)}, u32[]{:S(2)}) collective-permute-start(bf16[4,1,1,128,768]{4,3,2,1,0:T(8,128)(2,1)S(1)} %pad_maximum_fusion.refs_0_.refs_2_.refs_4_.refs_6_), channel_id=1, source_target_pairs={{0,4},{1,5},{2,6},{3,7},{4,0},{5,1},{6,2},{7,3},{8,12},{9,13},{10,... | collective-permute-start | bytes 2359304 | tf_op jit(solution)/shard_map/ppermute | solution.py:29
  72.1 19.7 %collective-permute-start.26 = (bf16[4,1,1,128,768]{4,3,2,1,0:T(8,128)(2,1)S(1)}, bf16[4,1,1,128,768]{4,3,2,1,0:T(8,128)(2,1)S(1)}, u32[]{:S(2)}, u32[]{:S(2)}) collective-permute-start(bf16[4,1,1,128,768]{4,3,2,1,0:T(8,128)(2,1)S(1)} %pad_maximum_fusion.refs_0_.refs_2_.refs_4_.refs_6_), channel_id=1, source_target_pairs={{0,2},{1,3},{2,0},{3,1},{4,6},{5,7},{6,4},{7,5},{8,10},{9,11},{10,... | collective-permute-start | bytes 2359304 | tf_op jit(solution)/shard_map/ppermute | solution.py:29
  75.4 16.4 %copy-start.7 = (f32[640,1]{0,1:T(1,128)S(1)}, f32[640,1]{0,1:T(1,128)}, u32[]{:S(2)}) copy-start(f32[640,1]{0,1:T(1,128)} %stack_reshape.12) | copy-start | bytes 7684
  90.3 1.5 copy-start.6
  91.7 18.4 %copy-start = (bf16[4,1,1,128,768]{4,3,2,1,0:T(8,128)(2,1)}, bf16[4,1,1,128,768]{4,3,2,1,0:T(8,128)(2,1)S(1)}, u32[]{:S(2)}) copy-start(bf16[4,1,1,128,768]{4,3,2,1,0:T(8,128)(2,1)S(1)} %collective-permute-done.26.refs_0_.refs_2_.refs_4_.refs_6_) | copy-start | bytes 2359300
  92.7 20.7 %collective-permute-start.27 = (bf16[2,1,1,128,768]{4,3,2,1,0:T(8,128)(2,1)S(1)}, bf16[2,1,1,128,768]{4,3,2,1,0:T(8,128)(2,1)S(1)}, u32[]{:S(2)}, u32[]{:S(2)}) collective-permute-start(bf16[2,1,1,128,768]{4,3,2,1,0:T(8,128)(2,1)S(1)} %slice.125), channel_id=1, source_target_pairs={{0,4},{1,5},{2,6},{3,7},{4,0},{5,1},{6,2},{7,3},{8,12},{9,13},{10,... | collective-permute-start | bytes 1179656 | tf_op jit(solution)/shard_map/ppermute | solution.py:29
  95.0 18.4 %collective-permute-start.28 = (bf16[2,1,1,128,768]{4,3,2,1,0:T(8,128)(2,1)S(1)}, bf16[2,1,1,128,768]{4,3,2,1,0:T(8,128)(2,1)S(1)}, u32[]{:S(2)}, u32[]{:S(2)}) collective-permute-start(bf16[2,1,1,128,768]{4,3,2,1,0:T(8,128)(2,1)S(1)} %slice.126), channel_id=1, source_target_pairs={{0,2},{1,3},{2,0},{3,1},{4,6},{5,7},{6,4},{7,5},{8,10},{9,11},{10,... | collective-permute-start | bytes 1179656 | tf_op jit(solution)/shard_map/ppermute | solution.py:29
  113.4 16.3 %collective-permute-start.31 = (bf16[8,128,768]{2,1,0:T(8,128)(2,1)}, bf16[8,128,768]{2,1,0:T(8,128)(2,1)S(1)}, u32[]{:S(2)}, u32[]{:S(2)}) collective-permute-start(bf16[8,128,768]{2,1,0:T(8,128)(2,1)} %bitcast.51), channel_id=1, source_target_pairs={{0,1},{1,0},{2,3},{3,2},{4,5},{5,4},{6,7},{7,6},{8,9},{9,8},{10,11... | collective-permute-start | bytes 4718600 | tf_op jit(solution)/shard_map/ppermute | solution.py:29
  113.4 13.7 %copy-start.2 = (bf16[2,1,1,128,768]{4,3,2,1,0:T(8,128)(2,1)}, bf16[2,1,1,128,768]{4,3,2,1,0:T(8,128)(2,1)S(1)}, u32[]{:S(2)}) copy-start(bf16[2,1,1,128,768]{4,3,2,1,0:T(8,128)(2,1)S(1)} %collective-permute-done.27.refs_1_.refs_3_) | copy-start | bytes 1179652
  113.4 13.6 %copy-start.3 = (bf16[2,1,1,128,768]{4,3,2,1,0:T(8,128)(2,1)}, bf16[2,1,1,128,768]{4,3,2,1,0:T(8,128)(2,1)S(1)}, u32[]{:S(2)}) copy-start(bf16[2,1,1,128,768]{4,3,2,1,0:T(8,128)(2,1)S(1)} %collective-permute-done.28.refs_5_.refs_7_) | copy-start | bytes 1179652
  129.2 15.0 %collective-permute-start.29 = (bf16[8,128,768]{2,1,0:T(8,128)(2,1)S(1)}, bf16[8,128,768]{2,1,0:T(8,128)(2,1)}, u32[]{:S(2)}, u32[]{:S(2)}) collective-permute-start(bf16[8,128,768]{2,1,0:T(8,128)(2,1)S(1)} %bitcast.219), channel_id=1, source_target_pairs={{0,1},{1,0},{2,3},{3,2},{4,5},{5,4},{6,7},{7,6},{8,9},{9,8},{10,11... | collective-permute-start | bytes 4718600 | tf_op jit(solution)/shard_map/ppermute | solution.py:29
  130.6 11.4 %collective-permute-start.32 = (bf16[4,64,768]{2,1,0:T(8,128)(2,1)}, bf16[4,64,768]{2,1,0:T(8,128)(2,1)}, u32[]{:S(2)}, u32[]{:S(2)}) collective-permute-start(bf16[4,64,768]{2,1,0:T(8,128)(2,1)} %fusion.34), channel_id=1, source_target_pairs={{0,4},{1,5},{2,6},{3,7},{4,0},{5,1},{6,2},{7,3},{8,12},{9,13},{10,... | collective-permute-start | bytes 1179656 | tf_op jit(solution)/shard_map/ppermute | solution.py:29
  131.6 20.6 %collective-permute-start.34 = (bf16[4,2,64,768]{3,2,0,1:T(8,128)(2,1)S(1)}, bf16[4,2,64,768]{3,2,0,1:T(8,128)(2,1)}, u32[]{:S(2)}, u32[]{:S(2)}) collective-permute-start(bf16[4,2,64,768]{3,2,0,1:T(8,128)(2,1)S(1)} %add_convert_fusion), channel_id=1, source_target_pairs={{0,2},{1,3},{2,0},{3,1},{4,6},{5,7},{6,4},{7,5},{8,10},{9,11},{10,... | collective-permute-start | bytes 2359304 | tf_op jit(solution)/shard_map/ppermute | solution.py:29
  136.5 27.8 %collective-permute-start.39 = (bf16[8,80,768]{2,1,0:T(8,128)(2,1)}, bf16[8,80,768]{2,1,0:T(8,128)(2,1)S(1)}, u32[]{:S(2)}, u32[]{:S(2)}) collective-permute-start(bf16[8,80,768]{2,1,0:T(8,128)(2,1)} %get-tuple-element.44), channel_id=1, source_target_pairs={{0,1},{1,0},{2,3},{3,2},{4,5},{5,4},{6,7},{7,6},{8,9},{9,8},{10,11... | collective-permute-start | bytes 2949128 | tf_op jit(solution)/shard_map/ppermute | solution.py:29
  140.7 14.0 %copy-start.9 = (f32[640]{0:T(1024)S(1)}, f32[640]{0:T(1024)}, u32[]{:S(2)}) copy-start(f32[640]{0:T(1024)} %reshape.180) | copy-start | bytes 7684
  140.7 14.0 %copy-start.10 = (bf16[8,80,3072]{2,1,0:T(8,128)(2,1)S(1)}, bf16[8,80,3072]{2,1,0:T(8,128)(2,1)}, u32[]{:S(2)}) copy-start(bf16[8,80,3072]{2,1,0:T(8,128)(2,1)} %constant_dynamic-update-slice_fusion.2) | copy-start | bytes 11796484
  140.7 23.7 %collective-permute-start.40 = (bf16[8,80,768]{2,1,0:T(8,128)(2,1)}, bf16[8,80,768]{2,1,0:T(8,128)(2,1)S(1)}, u32[]{:S(2)}, u32[]{:S(2)}) collective-permute-start(bf16[8,80,768]{2,1,0:T(8,128)(2,1)} %get-tuple-element.45), channel_id=1, source_target_pairs={{0,1},{1,0},{2,3},{3,2},{4,5},{5,4},{6,7},{7,6},{8,9},{9,8},{10,11... | collective-permute-start | bytes 2949128 | tf_op jit(solution)/shard_map/ppermute | solution.py:29
  143.1 21.5 %collective-permute-start.33 = (bf16[4,64,768]{2,1,0:T(8,128)(2,1)S(1)}, bf16[4,64,768]{2,1,0:T(8,128)(2,1)S(1)}, u32[]{:S(2)}, u32[]{:S(2)}) collective-permute-start(bf16[4,64,768]{2,1,0:T(8,128)(2,1)S(1)} %fusion.29), channel_id=1, source_target_pairs={{0,2},{1,3},{2,0},{3,1},{4,6},{5,7},{6,4},{7,5},{8,10},{9,11},{10,... | collective-permute-start | bytes 1179656 | tf_op jit(solution)/shard_map/ppermute | solution.py:29
  145.3 19.3 %collective-permute-start.30 = (bf16[4,64,768]{2,1,0:T(8,128)(2,1)S(1)}, bf16[4,64,768]{2,1,0:T(8,128)(2,1)S(1)}, u32[]{:S(2)}, u32[]{:S(2)}) collective-permute-start(bf16[4,64,768]{2,1,0:T(8,128)(2,1)S(1)} %fusion.32), channel_id=1, source_target_pairs={{0,4},{1,5},{2,6},{3,7},{4,0},{5,1},{6,2},{7,3},{8,12},{9,13},{10,... | collective-permute-start | bytes 1179656 | tf_op jit(solution)/shard_map/ppermute | solution.py:29
  153.4 10.9 %copy-start.1 = (bf16[8,80,3072]{2,1,0:T(8,128)(2,1)S(1)}, bf16[8,80,3072]{2,1,0:T(8,128)(2,1)}, u32[]{:S(2)}) copy-start(bf16[8,80,3072]{2,1,0:T(8,128)(2,1)} %get-tuple-element.43) | copy-start | bytes 11796484
  153.4 11.2 %collective-permute-start.35 = (bf16[4,64,768]{2,1,0:T(8,128)(2,1)S(1)}, bf16[4,64,768]{2,1,0:T(8,128)(2,1)S(1)}, u32[]{:S(2)}, u32[]{:S(2)}) collective-permute-start(bf16[4,64,768]{2,1,0:T(8,128)(2,1)S(1)} %fusion.36), channel_id=1, source_target_pairs={{0,4},{1,5},{2,6},{3,7},{4,0},{5,1},{6,2},{7,3},{8,12},{9,13},{10,... | collective-permute-start | bytes 1179656 | tf_op jit(solution)/shard_map/ppermute | solution.py:29
  164.6 3.0 %copy-start.22 = (bf16[640,1024]{1,0:T(8,128)(2,1)S(1)}, bf16[640,1024]{1,0:T(8,128)(2,1)}, u32[]{:S(2)}) copy-start(bf16[640,1024]{1,0:T(8,128)(2,1)} %get-tuple-element.38.da) | copy-start | bytes 3932164
  166.4 9.2 %collective-permute-start.36 = (bf16[128,768]{1,0:T(8,128)(2,1)S(1)}, bf16[128,768]{1,0:T(8,128)(2,1)S(1)}, u32[]{:S(2)}, u32[]{:S(2)}) collective-permute-start(bf16[128,768]{1,0:T(8,128)(2,1)S(1)} %pad_maximum_fusion.2), channel_id=1, source_target_pairs={{0,8},{1,9},{2,10},{3,11},{4,12},{5,13},{6,14},{7,15},{8,0},{9,1},... | collective-permute-start | bytes 589832 | tf_op jit(solution)/shard_map/ppermute | solution.py:29
  167.6 10.5 %copy-start.21 = (bf16[640,1024]{1,0:T(8,128)(2,1)S(1)}, bf16[640,1024]{1,0:T(8,128)(2,1)}, u32[]{:S(2)}) copy-start(bf16[640,1024]{1,0:T(8,128)(2,1)} %get-tuple-element.39.db) | copy-start | bytes 3932164
  174.6 10.5 %collective-permute-start.38 = (bf16[128,768]{1,0:T(8,128)(2,1)S(1)}, bf16[128,768]{1,0:T(8,128)(2,1)S(1)}, u32[]{:S(2)}, u32[]{:S(2)}) collective-permute-start(bf16[128,768]{1,0:T(8,128)(2,1)S(1)} %pad_maximum_fusion.3), channel_id=1, source_target_pairs={{0,8},{1,9},{2,10},{3,11},{4,12},{5,13},{6,14},{7,15},{8,0},{9,1},... | collective-permute-start | bytes 589832 | tf_op jit(solution)/shard_map/ppermute | solution.py:29
  175.7 9.7 %collective-permute-start.37 = (bf16[128,768]{1,0:T(8,128)(2,1)S(1)}, bf16[128,768]{1,0:T(8,128)(2,1)S(1)}, u32[]{:S(2)}, u32[]{:S(2)}) collective-permute-start(bf16[128,768]{1,0:T(8,128)(2,1)S(1)} %add_convert_fusion.11), channel_id=1, source_target_pairs={{0,16},{1,17},{2,18},{3,19},{4,20},{5,21},{6,22},{7,23},{8,24},{9,... | collective-permute-start | bytes 589832 | tf_op jit(solution)/shard_map/ppermute | solution.py:29

commit v2 on v1

--- a/solution.py
+++ b/solution.py
@@ -177,7 +177,9 @@
             scratch_shapes=scratch,
         ),
         input_output_aliases=aliases,
-        compiler_params=pltpu.CompilerParams(vmem_limit_bytes=56 * MIB),
+        compiler_params=pltpu.CompilerParams(
+            vmem_limit_bytes=(16 if dps <= 8 and sizes is None else 56) * MIB
+        ),
         cost_estimate=pl.CostEstimate(flops=4 * GFLOP // 2, bytes_accessed=16 * MIB, transcendentals=0),
         name=name,
     )(scalars, prefix_ids, *operands)

time: 187 us -> 179 us (0.957)
  Pallas kernels: 45.2 us -> 39.3 us
  waiting for transfers between devices: 21.8 us -> 27.2 us
  other arithmetic: 16.6 us -> 12.5 us
  matrix products: 35.7 us -> 33.6 us
    pallas_call x4, Pallas kernels: 17.8 us -> 11.9 us  [route(): pl.pallas_call(functools.partial(kernel, (dps, cap, *(sizes or ()))), out...]
    ppermute x41, waiting for transfers between devices: 21.8 us -> 27.2 us  [send(): return lax.ppermute(value, AXES, pairs)]
    convert_element_type x8, other arithmetic: 7.04 us -> 2.86 us  [add(): return total.astype(BF16)]
    dot_general x1, matrix products: 9.55 us -> 7.48 us  [body(): lax.dot_general(weighted, rows_g, tn, preferred_element_type=F32)]
  transfers between devices with their start and end apart: 41 -> 41, of which waited for: 12 -> 12; matrix products, arithmetic and copies ran while one was open for 32% -> 30% of each run, Pallas kernels for 24% -> 22%
where the time goes in v2:
time: 179 us; the launch traced here: 178 us
  starting transfers between devices  52.5 us (29%)
  Pallas kernels  39.3 us (22%)
  matrix products  33.6 us (19%)
  waiting for transfers between devices  27.2 us (15%)
  other arithmetic  12.5 us (7%)
  local copies, waits for them, and re-layouts  12.1 us (7%)
    ppermute x41, starting transfers between devices, send(): return lax.ppermute(value, AXES, pairs)  52.5 us
    pallas_call x2, Pallas kernels, dx_tokens(): pl.pallas_call(dx_kernel, out_shape=jax.ShapeDtypeStruct((2, all_tok, fea...  27.4 us
    ppermute x41, waiting for transfers between devices, send(): return lax.ppermute(value, AXES, pairs)  27.2 us
    pallas_call x4, Pallas kernels, route(): pl.pallas_call(functools.partial(kernel, (dps, cap, *(sizes or ()))), out...  11.9 us
    dot_general x1, matrix products, body(): lax.dot_general(rows_g, down_w, (((1,), (1,)), ((), ())), preferred_eleme...  10.7 us
    dot_general x1, matrix products, body(): lax.dot_general(weighted, rows_g, tn, preferred_element_type=F32)  7.48 us
    dot_general x1, matrix products, body(): grad_up = lax.dot_general(rows_x, d_b, tn, preferred_element_type=F32)  7.04 us
    dot_general x1, matrix products, body(): grad_gate = lax.dot_general(rows_x, d_a, tn, preferred_element_type=F32)  7.04 us
  transfers between devices with their start and end apart: 41, of which 12 were waited for; matrix products, arithmetic and copies ran while one was open for 30% of the time, Pallas kernels for 22%

profile of v2, /device:TPU:0, one launch (start us, length us, event | category | flops | bytes accessed | tf_op | source)
XLA Modules:
  0.0 178.3 jit_solution(4795868874192435595)
XLA Ops:
  0.6 1.8 fusion.37
  2.4 3.0 %collective-permute-start.1 = (bf16[1,1,192,768]{3,2,1,0:T(8,128)(2,1)S(1)}, bf16[1,1,192,768]{3,2,1,0:T(8,128)(2,1)S(1)}, u32[]{:S(2)}, u32[]{:S(2)}) collective-permute-start(bf16[1,1,192,768]{3,2,1,0:T(8,128)(2,1)S(1)} %get-tuple-element.71), channel_id=1, source_target_pairs={{0,8},{1,9},{2,10},{3,11},{4,12},{5,13},{6,14},{7,15},{8,0},{9,1},... | collective-permute-start | bytes 884744 | tf_op jit(solution)/shard_map/ppermute | solution.py:29
  5.4 2.6 %collective-permute-start.3 = (bf16[1,1,192,768]{3,2,1,0:T(8,128)(2,1)S(1)}, bf16[1,1,192,768]{3,2,1,0:T(8,128)(2,1)S(1)}, u32[]{:S(2)}, u32[]{:S(2)}) collective-permute-start(bf16[1,1,192,768]{3,2,1,0:T(8,128)(2,1)S(1)} %get-tuple-element.71), channel_id=1, source_target_pairs={{0,16},{1,17},{2,18},{3,19},{4,20},{5,21},{6,22},{7,23},{8,24},{9,... | collective-permute-start | bytes 884744 | tf_op jit(solution)/shard_map/ppermute | solution.py:29
  8.0 1.5 collective-permute-start.10
  9.6 1.5 collective-permute-start.11
  11.0 0.7 convert_bitcast_fusion.5
  11.7 1.1 fusion.75
  13.0 0.7 convert_bitcast_fusion.7
  13.7 0.7 convert_bitcast_fusion.6
  15.1 3.5 %collective-permute-done.1 = bf16[1,1,192,768]{3,2,1,0:T(8,128)(2,1)S(1)} collective-permute-done((bf16[1,1,192,768]{3,2,1,0:T(8,128)(2,1)S(1)}, bf16[1,1,192,768]{3,2,1,0:T(8,128)(2,1)S(1)}, u32[]{:S(2)}, u32[]{:S(2)}) %collective-permute-start.1) | collective-permute-done | bytes 294944 | tf_op jit(solution)/shard_map/ppermute | solution.py:29
  18.7 1.7 collective-permute-start.2
  21.6 1.5 collective-permute-start.7
  23.2 1.6 collective-permute-start.4
  25.4 1.5 collective-permute-done.4
  26.9 1.5 collective-permute-start.16
  28.4 0.8 collective-permute-done.7
  29.2 1.2 collective-permute-start.8
  30.3 0.9 collective-permute-start.6
  31.3 1.6 collective-permute-start.14
  32.9 1.5 collective-permute-start.12
  34.5 2.0 %collective-permute-done.6 = f32[2,8,128]{2,1,0:T(8,128)S(1)} collective-permute-done((f32[2,8,128]{2,1,0:T(8,128)S(1)}, f32[2,8,128]{2,1,0:T(8,128)S(1)}, u32[]{:S(2)}, u32[]{:S(2)}) %collective-permute-start.6) | collective-permute-done | bytes 8224 | tf_op jit(solution)/shard_map/ppermute | solution.py:29
  36.5 1.6 collective-permute-start.13
  38.1 1.6 collective-permute-start.9
  40.3 1.4 collective-permute-start.17
  41.8 1.1 collective-permute-done.9
  42.9 1.5 collective-permute-start.19
  45.5 0.8 add_convert_fusion.9.refs_8_
  46.3 3.0 %collective-permute-start.23 = (bf16[1,1,128,768]{3,2,1,0:T(8,128)(2,1)S(1)}, bf16[1,1,128,768]{3,2,1,0:T(8,128)(2,1)S(1)}, u32[]{:S(2)}, u32[]{:S(2)}) collective-permute-start(bf16[1,1,128,768]{3,2,1,0:T(8,128)(2,1)S(1)} %bitcast.223), channel_id=1, source_target_pairs={{0,16},{1,17},{2,18},{3,19},{4,20},{5,21},{6,22},{7,23},{8,24},{9,... | collective-permute-start | bytes 589832 | tf_op jit(solution)/shard_map/ppermute | solution.py:29
  49.4 1.1 collective-permute-start.15
  50.4 2.1 %collective-permute-start.18 = (bf16[1,1,192,768]{3,2,1,0:T(8,128)(2,1)}, bf16[1,1,192,768]{3,2,1,0:T(8,128)(2,1)}, u32[]{:S(2)}, u32[]{:S(2)}) collective-permute-start(bf16[1,1,192,768]{3,2,1,0:T(8,128)(2,1)} %collective-permute-done.17), channel_id=1, source_target_pairs={{0,8},{1,9},{2,10},{3,11},{4,12},{5,13},{6,14},{7,15},{8,0},{9,1},... | collective-permute-start | bytes 884744 | tf_op jit(solution)/shard_map/ppermute | solution.py:29
  53.2 4.7 %route_g.2 = (bf16[8,80,3072]{2,1,0:T(8,128)(2,1)}, bf16[8,80,768]{2,1,0:T(8,128)(2,1)}) custom-call(s32[2]{0:T(128)} %pad_add_fusion.2.my_ref, s32[32]{0:T(128)} %convert_element_type.338.pid_ref, bf16[1,1,1,192,768]{4,3,2,1,0:T(8,128)(2,1)} %get-tuple-element.70.refs_0_, bf16[1,1,1,192,768]{4,3,2,1,0:T(8,128)(2,1)} %bitcast.252, ...), custom_call_target="tpu_custom_call" | custom-call | flops 2000000000 | bytes 16777216 | tf_op jit(solution)/shard_map/route_g/pallas_call | solution.py:166
  58.0 2.0 %collective-permute-start.24 = (bf16[1,1,128,768]{3,2,1,0:T(8,128)(2,1)S(1)}, bf16[1,1,128,768]{3,2,1,0:T(8,128)(2,1)S(1)}, u32[]{:S(2)}, u32[]{:S(2)}) collective-permute-start(bf16[1,1,128,768]{3,2,1,0:T(8,128)(2,1)S(1)} %collective-permute-done.23), channel_id=1, source_target_pairs={{0,8},{1,9},{2,10},{3,11},{4,12},{5,13},{6,14},{7,15},{8,0},{9,1},... | collective-permute-start | bytes 589832 | tf_op jit(solution)/shard_map/ppermute | solution.py:29
  60.2 4.7 %route_g.3 = (bf16[8,80,3072]{2,1,0:T(8,128)(2,1)}, bf16[8,80,768]{2,1,0:T(8,128)(2,1)}) custom-call(s32[2]{0:T(128)} %pad_add_fusion.1.my_ref, s32[32]{0:T(128)} %convert_element_type.338.pid_ref, bf16[1,1,1,192,768]{4,3,2,1,0:T(8,128)(2,1)} %bitcast.249, bf16[1,1,1,192,768]{4,3,2,1,0:T(8,128)(2,1)} %bitcast.257, ...), custom_call_target="tpu_custom_call", output_to_operand_aliasing={{0}: (11, {})} | custom-call | flops 2000000000 | bytes 16777216 | tf_op jit(solution)/shard_map/route_g/pallas_call | solution.py:166
  65.2 0.8 select_reduce_fusion.3
  67.0 1.1 fusion.21.tokens_of
  68.2 2.7 %collective-permute-start.25 = (bf16[4,1,1,128,768]{4,3,2,1,0:T(8,128)(2,1)S(1)}, bf16[4,1,1,128,768]{4,3,2,1,0:T(8,128)(2,1)S(1)}, u32[]{:S(2)}, u32[]{:S(2)}) collective-permute-start(bf16[4,1,1,128,768]{4,3,2,1,0:T(8,128)(2,1)S(1)} %pad_maximum_fusion.refs_0_.refs_2_.refs_4_.refs_6_), channel_id=1, source_target_pairs={{0,4},{1,5},{2,6},{3,7},{4,0},{5,1},{6,2},{7,3},{8,12},{9,13},{10,... | collective-permute-start | bytes 2359304 | tf_op jit(solution)/shard_map/ppermute | solution.py:29
  70.9 1.3 collective-permute-start.26
  72.2 1.0 constant_dynamic-update-slice_fusion.3
  73.2 2.2 %constant_dynamic-update-slice_fusion.2 = bf16[8,80,3072]{2,1,0:T(8,128)(2,1)} fusion(bf16[8,80,3072]{2,1,0:T(8,128)(2,1)} %constant_dynamic-update-slice_fusion.3, bf16[8,80,768]{2,1,0:T(8,128)(2,1)} %collective-permute-done.21, s32[]{:T(128)S(6)} %select_n.107), kind=kLoop, calls=%fused_computation.170 | loop fusion | bytes 1966084 | tf_op jit(solution)/shard_map/dynamic_update_slice | solution.py:196
  75.4 10.7 %fusion.10 = (f32[640]{0:T(1024)S(1)}, bf16[640,1024]{1,0:T(8,128)(2,1)}, bf16[640,1024]{1,0:T(8,128)(2,1)}) fusion(bf16[1,640,1024]{2,1,0:T(8,128)(2,1)S(1)} %copy-done.7, bf16[1,640,1024]{2,1,0:T(8,128)(2,1)S(1)} %copy-done.9, f32[640]{0:T(1024)S(1)} %reshape.180, bf16[640,3072]{1,0:T(8,128)(2,1)} %bitcast.247, bf16[1,1024,3072]{2,1,0:T(8,128)(2,1)} %param.19), kind=kOutput, calls=%fused_computation.20 | convolution fusion | flops 4038983168 | bytes 15471616 | tf_op jit(solution)/shard_map/dot_general | solution.py:382
  86.1 3.0 %collective-permute-done.25.refs_1_.refs_3_.refs_5_.refs_7_ = bf16[4,1,1,128,768]{4,3,2,1,0:T(8,128)(2,1)S(1)} collective-permute-done((bf16[4,1,1,128,768]{4,3,2,1,0:T(8,128)(2,1)S(1)}, bf16[4,1,1,128,768]{4,3,2,1,0:T(8,128)(2,1)S(1)}, u32[]{:S(2)}, u32[]{:S(2)}) %collective-permute-start.25) | collective-permute-done | bytes 786464 | tf_op jit(solution)/shard_map/ppermute | solution.py:29
  89.1 1.5 collective-permute-done.26.refs_0_.refs_2_.refs_4_.refs_6_
  90.6 0.8 copy.41.dl
  91.9 1.5 collective-permute-start.28
  93.4 13.8 %dx.3 = bf16[2,1024,768]{2,1,0:T(8,128)(2,1)} custom-call(s32[2]{0:T(128)} %pad_add_fusion.my_ref, bf16[640,1024]{1,0:T(8,128)(2,1)} %get-tuple-element.38.da, bf16[640,1024]{1,0:T(8,128)(2,1)} %get-tuple-element.39.db, bf16[640,8]{1,0:T(8,128)(2,1)} %copy.41.dl, bf16[3072,1024]{1,0:T(8,128)(2,1)} %bitcast.243, bf16[3072,1024]{1,0:T(8,128)(2,1)} %bitcast.245, ...), custom_call_target="tpu_custom_call" | custom-call | flops 12000000000 | bytes 12582912 | tf_op jit(solution)/shard_map/dx/pallas_call | solution.py:221
  107.2 3.2 %fusion.73 = (bf16[1,1024,768]{2,1,0:T(8,128)(2,1)S(1)}, bf16[1,1024,768]{2,1,0:T(8,128)(2,1)}) fusion(bf16[2,1024,768]{2,1,0:T(8,128)(2,1)} %dx.3), kind=kLoop, calls=%fused_computation.185 | loop fusion | bytes 6291456 | tf_op jit(solution)/shard_map/slice | solution.py:404
  110.5 13.6 %dx.2 = bf16[2,1024,768]{2,1,0:T(8,128)(2,1)} custom-call(s32[2]{0:T(128)} %pad_add_fusion.my_ref, bf16[640,1024]{1,0:T(8,128)(2,1)} %get-tuple-element.38.da, bf16[640,1024]{1,0:T(8,128)(2,1)} %get-tuple-element.39.db, bf16[640,8]{1,0:T(8,128)(2,1)} %copy.41.dl, bf16[3072,1024]{1,0:T(8,128)(2,1)} %bitcast.244, bf16[3072,1024]{1,0:T(8,128)(2,1)} %bitcast.246, ...), custom_call_target="tpu_custom_call" | custom-call | flops 12000000000 | bytes 12582912 | tf_op jit(solution)/shard_map/dx/pallas_call | solution.py:221
  124.1 2.1 %fusion.72 = (bf16[1,1024,768]{2,1,0:T(8,128)(2,1)S(1)}, bf16[1,1024,768]{2,1,0:T(8,128)(2,1)S(1)}) fusion(bf16[2,1024,768]{2,1,0:T(8,128)(2,1)} %dx.2), kind=kLoop, calls=%fused_computation.184 | loop fusion | bytes 6291456 | tf_op jit(solution)/shard_map/slice | solution.py:404
  126.9 1.6 collective-permute-start.32
  128.6 0.8 collective-permute-start.34
  129.5 1.2 route_x.2
  130.8 1.3 route_x.3
  132.7 5.3 %collective-permute-done.32 = bf16[4,64,768]{2,1,0:T(8,128)(2,1)S(1)} collective-permute-done((bf16[4,64,768]{2,1,0:T(8,128)(2,1)S(1)}, bf16[4,64,768]{2,1,0:T(8,128)(2,1)S(1)}, u32[]{:S(2)}, u32[]{:S(2)}) %collective-permute-start.32) | collective-permute-done | bytes 393248 | tf_op jit(solution)/shard_map/ppermute | solution.py:29
  138.0 1.1 fusion.29
  139.9 1.7 collective-permute-start.30
  141.6 7.5 %collective-permute-done.34 = bf16[4,2,64,768]{3,2,0,1:T(8,128)(2,1)S(1)} collective-permute-done((bf16[4,2,64,768]{3,2,0,1:T(8,128)(2,1)S(1)}, bf16[4,2,64,768]{3,2,0,1:T(8,128)(2,1)S(1)}, u32[]{:S(2)}, u32[]{:S(2)}) %collective-permute-start.34) | collective-permute-done | bytes 786464 | tf_op jit(solution)/shard_map/ppermute | solution.py:29
  149.3 0.7 collective-permute-start.35
  150.0 7.5 %convert_bitcast_fusion = bf16[1,1024,3072]{2,1,0:T(8,128)(2,1)} fusion(bf16[640,3072]{1,0:T(8,128)(2,1)S(1)} %bitcast.248, bf16[1,640,1024]{2,1,0:T(8,128)(2,1)S(1)} %copy-done.8, bf16[1,640,1024]{2,1,0:T(8,128)(2,1)S(1)} %copy-done.10, f32[640]{0:T(1024)S(1)} %reshape.180), kind=kOutput, calls=%fused_computation.4 | convolution fusion | flops 4035575808 | bytes 12847616 | tf_op jit(solution)/shard_map/dot_general | solution.py:413
  158.8 1.3 collective-permute-start.36
  160.1 7.0 %convert_bitcast_fusion.2 = bf16[1,3072,1024]{2,1,0:T(8,128)(2,1)} fusion(bf16[640,3072]{1,0:T(8,128)(2,1)S(1)} %bitcast.208, bf16[640,1024]{1,0:T(8,128)(2,1)S(1)} %copy-done.21), kind=kOutput, calls=%fused_computation.6 | convolution fusion | flops 4029677568 | bytes 11534336 | tf_op jit(solution)/shard_map/dot_general | solution.py:414
  167.2 0.9 collective-permute-start.38
  168.1 2.4 %collective-permute-start.37 = (bf16[128,768]{1,0:T(8,128)(2,1)S(1)}, bf16[128,768]{1,0:T(8,128)(2,1)S(1)}, u32[]{:S(2)}, u32[]{:S(2)}) collective-permute-start(bf16[128,768]{1,0:T(8,128)(2,1)S(1)} %add_convert_fusion.11), channel_id=1, source_target_pairs={{0,16},{1,17},{2,18},{3,19},{4,20},{5,21},{6,22},{7,23},{8,24},{9,... | collective-permute-start | bytes 589832 | tf_op jit(solution)/shard_map/ppermute | solution.py:29
  170.5 7.0 %convert_bitcast_fusion.1 = bf16[1,3072,1024]{2,1,0:T(8,128)(2,1)} fusion(bf16[640,3072]{1,0:T(8,128)(2,1)S(1)} %bitcast.209, bf16[640,1024]{1,0:T(8,128)(2,1)S(1)} %copy-done.20), kind=kOutput, calls=%fused_computation.5 | convolution fusion | flops 4029677568 | bytes 11534336 | tf_op jit(solution)/shard_map/dot_general | solution.py:415
  177.6 0.8 add_convert_fusion.10
  (148 shorter events, 11.2 us)
Async XLA Ops:
  0.6 45.7 %copy-start.5 = (bf16[128,768]{1,0:T(8,128)(2,1)S(1)}, bf16[128,768]{1,0:T(8,128)(2,1)}, u32[]{:S(2)}) copy-start(bf16[128,768]{1,0:T(8,128)(2,1)} %param.11) | copy-start | bytes 589828
  2.4 16.2 %collective-permute-start.1 = (bf16[1,1,192,768]{3,2,1,0:T(8,128)(2,1)S(1)}, bf16[1,1,192,768]{3,2,1,0:T(8,128)(2,1)S(1)}, u32[]{:S(2)}, u32[]{:S(2)}) collective-permute-start(bf16[1,1,192,768]{3,2,1,0:T(8,128)(2,1)S(1)} %get-tuple-element.71), channel_id=1, source_target_pairs={{0,8},{1,9},{2,10},{3,11},{4,12},{5,13},{6,14},{7,15},{8,0},{9,1},... | collective-permute-start | bytes 884744 | tf_op jit(solution)/shard_map/ppermute | solution.py:29
  5.4 15.7 %collective-permute-start.3 = (bf16[1,1,192,768]{3,2,1,0:T(8,128)(2,1)S(1)}, bf16[1,1,192,768]{3,2,1,0:T(8,128)(2,1)S(1)}, u32[]{:S(2)}, u32[]{:S(2)}) collective-permute-start(bf16[1,1,192,768]{3,2,1,0:T(8,128)(2,1)S(1)} %get-tuple-element.71), channel_id=1, source_target_pairs={{0,16},{1,17},{2,18},{3,19},{4,20},{5,21},{6,22},{7,23},{8,24},{9,... | collective-permute-start | bytes 884744 | tf_op jit(solution)/shard_map/ppermute | solution.py:29
  8.0 23.3 %collective-permute-start.10 = (bf16[1,1,192,768]{3,2,1,0:T(8,128)(2,1)S(1)}, bf16[1,1,192,768]{3,2,1,0:T(8,128)(2,1)S(1)}, u32[]{:S(2)}, u32[]{:S(2)}) collective-permute-start(bf16[1,1,192,768]{3,2,1,0:T(8,128)(2,1)S(1)} %get-tuple-element.71), channel_id=1, source_target_pairs={{0,2},{1,3},{2,0},{3,1},{4,6},{5,7},{6,4},{7,5},{8,10},{9,11},{10,... | collective-permute-start | bytes 884744 | tf_op jit(solution)/shard_map/ppermute | solution.py:29
  9.6 23.4 %collective-permute-start.11 = (bf16[1,1,192,768]{3,2,1,0:T(8,128)(2,1)S(1)}, bf16[1,1,192,768]{3,2,1,0:T(8,128)(2,1)S(1)}, u32[]{:S(2)}, u32[]{:S(2)}) collective-permute-start(bf16[1,1,192,768]{3,2,1,0:T(8,128)(2,1)S(1)} %get-tuple-element.71), channel_id=1, source_target_pairs={{0,4},{1,5},{2,6},{3,7},{4,0},{5,1},{6,2},{7,3},{8,12},{9,13},{10,... | collective-permute-start | bytes 884744 | tf_op jit(solution)/shard_map/ppermute | solution.py:29
  12.9 2.2 %collective-permute-start = (f32[8,768]{1,0:T(8,128)S(1)}, f32[8,768]{1,0:T(8,128)S(1)}, u32[]{:S(2)}, u32[]{:S(2)}) collective-permute-start(f32[8,768]{1,0:T(8,128)S(1)} %select_maximum_fusion.1), channel_id=1, source_target_pairs={{0,1},{1,0},{2,3},{3,2},{4,5},{5,4},{6,7},{7,6},{8,9},{9,8},{10,11... | collective-permute-start | bytes 73736 | tf_op jit(solution)/shard_map/ppermute | solution.py:29
  18.7 34.5 %copy-start.12 = (bf16[1,1,192,768]{3,2,1,0:T(8,128)(2,1)}, bf16[1,1,192,768]{3,2,1,0:T(8,128)(2,1)S(1)}, u32[]{:S(2)}) copy-start(bf16[1,1,192,768]{3,2,1,0:T(8,128)(2,1)S(1)} %collective-permute-done.1) | copy-start | bytes 884740
  18.7 4.5 %collective-permute-start.2 = (f32[12,768]{1,0:T(8,128)S(1)}, f32[12,768]{1,0:T(8,128)S(1)}, u32[]{:S(2)}, u32[]{:S(2)}) collective-permute-start(f32[12,768]{1,0:T(8,128)S(1)} %fusion.41), channel_id=1, source_target_pairs={{0,2},{1,3},{2,0},{3,1},{4,6},{5,7},{6,4},{7,5},{8,10},{9,11},{10,... | collective-permute-start | bytes 110600 | tf_op jit(solution)/shard_map/ppermute | solution.py:29
  21.2 32.0 %copy-start.13 = (bf16[1,1,192,768]{3,2,1,0:T(8,128)(2,1)}, bf16[1,1,192,768]{3,2,1,0:T(8,128)(2,1)S(1)}, u32[]{:S(2)}) copy-start(bf16[1,1,192,768]{3,2,1,0:T(8,128)(2,1)S(1)} %collective-permute-done.3) | copy-start | bytes 884740
  21.2 9.2 %collective-permute-start.5 = (bf16[1,1,192,768]{3,2,1,0:T(8,128)(2,1)S(1)}, bf16[1,1,192,768]{3,2,1,0:T(8,128)(2,1)S(1)}, u32[]{:S(2)}, u32[]{:S(2)}) collective-permute-start(bf16[1,1,192,768]{3,2,1,0:T(8,128)(2,1)S(1)} %collective-permute-done.3), channel_id=1, source_target_pairs={{0,8},{1,9},{2,10},{3,11},{4,12},{5,13},{6,14},{7,15},{8,0},{9,1},... | collective-permute-start | bytes 884744 | tf_op jit(solution)/shard_map/ppermute | solution.py:29
  21.6 7.5 %collective-permute-start.7 = (bf16[1,1,192,768]{3,2,1,0:T(8,128)(2,1)S(1)}, bf16[1,1,192,768]{3,2,1,0:T(8,128)(2,1)S(1)}, u32[]{:S(2)}, u32[]{:S(2)}) collective-permute-start(bf16[1,1,192,768]{3,2,1,0:T(8,128)(2,1)S(1)} %collective-permute-done.3), channel_id=1, source_target_pairs={{0,2},{1,3},{2,0},{3,1},{4,6},{5,7},{6,4},{7,5},{8,10},{9,11},{10,... | collective-permute-start | bytes 884744 | tf_op jit(solution)/shard_map/ppermute | solution.py:29
  23.2 3.7 %collective-permute-start.4 = (f32[1,8,128]{2,1,0:T(8,128)S(1)}, f32[1,8,128]{2,1,0:T(8,128)S(1)}, u32[]{:S(2)}, u32[]{:S(2)}) collective-permute-start(f32[1,8,128]{2,1,0:T(8,128)S(1)} %pad_bitcast_fusion), channel_id=1, source_target_pairs={{0,4},{1,5},{2,6},{3,7},{4,0},{5,1},{6,2},{7,3},{8,12},{9,13},{10,... | collective-permute-start | bytes 12296 | tf_op jit(solution)/shard_map/ppermute | solution.py:29
  26.9 13.4 %collective-permute-start.16 = (bf16[1,1,192,768]{3,2,1,0:T(8,128)(2,1)S(1)}, bf16[1,1,192,768]{3,2,1,0:T(8,128)(2,1)S(1)}, u32[]{:S(2)}, u32[]{:S(2)}) collective-permute-start(bf16[1,1,192,768]{3,2,1,0:T(8,128)(2,1)S(1)} %collective-permute-done.3), channel_id=1, source_target_pairs={{0,4},{1,5},{2,6},{3,7},{4,0},{5,1},{6,2},{7,3},{8,12},{9,13},{10,... | collective-permute-start | bytes 884744 | tf_op jit(solution)/shard_map/ppermute | solution.py:29
  29.2 15.9 %copy-start.15 = (bf16[1,1,192,768]{3,2,1,0:T(8,128)(2,1)}, bf16[1,1,192,768]{3,2,1,0:T(8,128)(2,1)S(1)}, u32[]{:S(2)}) copy-start(bf16[1,1,192,768]{3,2,1,0:T(8,128)(2,1)S(1)} %collective-permute-done.7) | copy-start | bytes 884740
  29.2 8.9 %collective-permute-start.8 = (bf16[1,1,192,768]{3,2,1,0:T(8,128)(2,1)S(1)}, bf16[1,1,192,768]{3,2,1,0:T(8,128)(2,1)S(1)}, u32[]{:S(2)}, u32[]{:S(2)}) collective-permute-start(bf16[1,1,192,768]{3,2,1,0:T(8,128)(2,1)S(1)} %collective-permute-done.7), channel_id=1, source_target_pairs={{0,8},{1,9},{2,10},{3,11},{4,12},{5,13},{6,14},{7,15},{8,0},{9,1},... | collective-permute-start | bytes 884744 | tf_op jit(solution)/shard_map/ppermute | solution.py:29
  30.3 22.8 %copy-start.16 = (bf16[1,1,192,768]{3,2,1,0:T(8,128)(2,1)}, bf16[1,1,192,768]{3,2,1,0:T(8,128)(2,1)S(1)}, u32[]{:S(2)}) copy-start(bf16[1,1,192,768]{3,2,1,0:T(8,128)(2,1)S(1)} %collective-permute-done.5) | copy-start | bytes 884740
  30.3 6.1 %collective-permute-start.6 = (f32[2,8,128]{2,1,0:T(8,128)S(1)}, f32[2,8,128]{2,1,0:T(8,128)S(1)}, u32[]{:S(2)}, u32[]{:S(2)}) collective-permute-start(f32[2,8,128]{2,1,0:T(8,128)S(1)} %pad_maximum_fusion.8), channel_id=1, source_target_pairs={{0,8},{1,9},{2,10},{3,11},{4,12},{5,13},{6,14},{7,15},{8,0},{9,1},... | collective-permute-start | bytes 24584 | tf_op jit(solution)/shard_map/ppermute | solution.py:29
  31.3 26.5 %copy-start.11 = (bf16[1,1,192,768]{3,2,1,0:T(8,128)(2,1)}, bf16[1,1,192,768]{3,2,1,0:T(8,128)(2,1)S(1)}, u32[]{:S(2)}) copy-start(bf16[1,1,192,768]{3,2,1,0:T(8,128)(2,1)S(1)} %collective-permute-done.10) | copy-start | bytes 884740
  31.3 15.0 %collective-permute-start.14 = (bf16[1,1,192,768]{3,2,1,0:T(8,128)(2,1)S(1)}, bf16[1,1,192,768]{3,2,1,0:T(8,128)(2,1)}, u32[]{:S(2)}, u32[]{:S(2)}) collective-permute-start(bf16[1,1,192,768]{3,2,1,0:T(8,128)(2,1)S(1)} %collective-permute-done.1), channel_id=1, source_target_pairs={{0,4},{1,5},{2,6},{3,7},{4,0},{5,1},{6,2},{7,3},{8,12},{9,13},{10,... | collective-permute-start | bytes 884744 | tf_op jit(solution)/shard_map/ppermute | solution.py:29
  32.9 20.2 %copy-start.14 = (bf16[1,1,192,768]{3,2,1,0:T(8,128)(2,1)}, bf16[1,1,192,768]{3,2,1,0:T(8,128)(2,1)S(1)}, u32[]{:S(2)}) copy-start(bf16[1,1,192,768]{3,2,1,0:T(8,128)(2,1)S(1)} %collective-permute-done.11) | copy-start | bytes 884740
  32.9 24.9 %collective-permute-start.12 = (bf16[1,1,192,768]{3,2,1,0:T(8,128)(2,1)S(1)}, bf16[1,1,192,768]{3,2,1,0:T(8,128)(2,1)S(1)}, u32[]{:S(2)}, u32[]{:S(2)}) collective-permute-start(bf16[1,1,192,768]{3,2,1,0:T(8,128)(2,1)S(1)} %collective-permute-done.11), channel_id=1, source_target_pairs={{0,2},{1,3},{2,0},{3,1},{4,6},{5,7},{6,4},{7,5},{8,10},{9,11},{10,... | collective-permute-start | bytes 884744 | tf_op jit(solution)/shard_map/ppermute | solution.py:29
  36.5 23.5 %collective-permute-start.13 = (bf16[1,1,192,768]{3,2,1,0:T(8,128)(2,1)S(1)}, bf16[1,1,192,768]{3,2,1,0:T(8,128)(2,1)}, u32[]{:S(2)}, u32[]{:S(2)}) collective-permute-start(bf16[1,1,192,768]{3,2,1,0:T(8,128)(2,1)S(1)} %collective-permute-done.10), channel_id=1, source_target_pairs={{0,8},{1,9},{2,10},{3,11},{4,12},{5,13},{6,14},{7,15},{8,0},{9,1},... | collective-permute-start | bytes 884744 | tf_op jit(solution)/shard_map/ppermute | solution.py:29
  38.1 19.8 %copy-start.17 = (bf16[1,1,192,768]{3,2,1,0:T(8,128)(2,1)}, bf16[1,1,192,768]{3,2,1,0:T(8,128)(2,1)S(1)}, u32[]{:S(2)}) copy-start(bf16[1,1,192,768]{3,2,1,0:T(8,128)(2,1)S(1)} %collective-permute-done.8) | copy-start | bytes 884740
  38.1 4.8 %collective-permute-start.9 = (f32[4,8,128]{2,1,0:T(8,128)S(1)}, f32[4,8,128]{2,1,0:T(8,128)S(1)}, u32[]{:S(2)}, u32[]{:S(2)}) collective-permute-start(f32[4,8,128]{2,1,0:T(8,128)S(1)} %pad_maximum_fusion.6), channel_id=1, source_target_pairs={{0,16},{1,17},{2,18},{3,19},{4,20},{5,21},{6,22},{7,23},{8,24},{9,... | collective-permute-start | bytes 49160 | tf_op jit(solution)/shard_map/ppermute | solution.py:29
  40.3 12.8 %copy-start.18 = (bf16[1,1,192,768]{3,2,1,0:T(8,128)(2,1)}, bf16[1,1,192,768]{3,2,1,0:T(8,128)(2,1)S(1)}, u32[]{:S(2)}) copy-start(bf16[1,1,192,768]{3,2,1,0:T(8,128)(2,1)S(1)} %collective-permute-done.16) | copy-start | bytes 884740
  40.3 9.0 %collective-permute-start.17 = (bf16[1,1,192,768]{3,2,1,0:T(8,128)(2,1)S(1)}, bf16[1,1,192,768]{3,2,1,0:T(8,128)(2,1)}, u32[]{:S(2)}, u32[]{:S(2)}) collective-permute-start(bf16[1,1,192,768]{3,2,1,0:T(8,128)(2,1)S(1)} %collective-permute-done.16), channel_id=1, source_target_pairs={{0,2},{1,3},{2,0},{3,1},{4,6},{5,7},{6,4},{7,5},{8,10},{9,11},{10,... | collective-permute-start | bytes 884744 | tf_op jit(solution)/shard_map/ppermute | solution.py:29
  42.9 7.6 %collective-permute-start.19 = (bf16[1,1,192,768]{3,2,1,0:T(8,128)(2,1)S(1)}, bf16[1,1,192,768]{3,2,1,0:T(8,128)(2,1)}, u32[]{:S(2)}, u32[]{:S(2)}) collective-permute-start(bf16[1,1,192,768]{3,2,1,0:T(8,128)(2,1)S(1)} %collective-permute-done.5), channel_id=1, source_target_pairs={{0,4},{1,5},{2,6},{3,7},{4,0},{5,1},{6,2},{7,3},{8,12},{9,13},{10,... | collective-permute-start | bytes 884744 | tf_op jit(solution)/shard_map/ppermute | solution.py:29
  46.3 11.7 %collective-permute-start.23 = (bf16[1,1,128,768]{3,2,1,0:T(8,128)(2,1)S(1)}, bf16[1,1,128,768]{3,2,1,0:T(8,128)(2,1)S(1)}, u32[]{:S(2)}, u32[]{:S(2)}) collective-permute-start(bf16[1,1,128,768]{3,2,1,0:T(8,128)(2,1)S(1)} %bitcast.223), channel_id=1, source_target_pairs={{0,16},{1,17},{2,18},{3,19},{4,20},{5,21},{6,22},{7,23},{8,24},{9,... | collective-permute-start | bytes 589832 | tf_op jit(solution)/shard_map/ppermute | solution.py:29
  49.4 10.6 %collective-permute-start.15 = (bf16[1,1,192,768]{3,2,1,0:T(8,128)(2,1)}, bf16[1,1,192,768]{3,2,1,0:T(8,128)(2,1)}, u32[]{:S(2)}, u32[]{:S(2)}) collective-permute-start(bf16[1,1,192,768]{3,2,1,0:T(8,128)(2,1)} %collective-permute-done.14), channel_id=1, source_target_pairs={{0,2},{1,3},{2,0},{3,1},{4,6},{5,7},{6,4},{7,5},{8,10},{9,11},{10,... | collective-permute-start | bytes 884744 | tf_op jit(solution)/shard_map/ppermute | solution.py:29
  50.4 9.8 %collective-permute-start.18 = (bf16[1,1,192,768]{3,2,1,0:T(8,128)(2,1)}, bf16[1,1,192,768]{3,2,1,0:T(8,128)(2,1)}, u32[]{:S(2)}, u32[]{:S(2)}) collective-permute-start(bf16[1,1,192,768]{3,2,1,0:T(8,128)(2,1)} %collective-permute-done.17), channel_id=1, source_target_pairs={{0,8},{1,9},{2,10},{3,11},{4,12},{5,13},{6,14},{7,15},{8,0},{9,1},... | collective-permute-start | bytes 884744 | tf_op jit(solution)/shard_map/ppermute | solution.py:29
  57.9 2.1 %copy-start.19 = (bf16[1,1,192,768]{3,2,1,0:T(8,128)(2,1)}, bf16[1,1,192,768]{3,2,1,0:T(8,128)(2,1)S(1)}, u32[]{:S(2)}) copy-start(bf16[1,1,192,768]{3,2,1,0:T(8,128)(2,1)S(1)} %collective-permute-done.12) | copy-start | bytes 884740
  57.9 10.2 %collective-permute-start.22 = (bf16[1,1,128,768]{3,2,1,0:T(8,128)(2,1)S(1)}, bf16[1,1,128,768]{3,2,1,0:T(8,128)(2,1)S(1)}, u32[]{:S(2)}, u32[]{:S(2)}) collective-permute-start(bf16[1,1,128,768]{3,2,1,0:T(8,128)(2,1)S(1)} %bitcast.224), channel_id=1, source_target_pairs={{0,8},{1,9},{2,10},{3,11},{4,12},{5,13},{6,14},{7,15},{8,0},{9,1},... | collective-permute-start | bytes 589832 | tf_op jit(solution)/shard_map/ppermute | solution.py:29
  58.0 10.1 %collective-permute-start.24 = (bf16[1,1,128,768]{3,2,1,0:T(8,128)(2,1)S(1)}, bf16[1,1,128,768]{3,2,1,0:T(8,128)(2,1)S(1)}, u32[]{:S(2)}, u32[]{:S(2)}) collective-permute-start(bf16[1,1,128,768]{3,2,1,0:T(8,128)(2,1)S(1)} %collective-permute-done.23), channel_id=1, source_target_pairs={{0,8},{1,9},{2,10},{3,11},{4,12},{5,13},{6,14},{7,15},{8,0},{9,1},... | collective-permute-start | bytes 589832 | tf_op jit(solution)/shard_map/ppermute | solution.py:29
  60.0 12.2 %collective-permute-start.20 = (bf16[8,80,768]{2,1,0:T(8,128)(2,1)}, bf16[8,80,768]{2,1,0:T(8,128)(2,1)S(1)}, u32[]{:S(2)}, u32[]{:S(2)}) collective-permute-start(bf16[8,80,768]{2,1,0:T(8,128)(2,1)} %get-tuple-element.31), channel_id=1, source_target_pairs={{0,1},{1,0},{2,3},{3,2},{4,5},{5,4},{6,7},{7,6},{8,9},{9,8},{10,11... | collective-permute-start | bytes 2949128 | tf_op jit(solution)/shard_map/ppermute | solution.py:29
  64.9 8.3 %collective-permute-start.21 = (bf16[8,80,768]{2,1,0:T(8,128)(2,1)}, bf16[8,80,768]{2,1,0:T(8,128)(2,1)}, u32[]{:S(2)}, u32[]{:S(2)}) collective-permute-start(bf16[8,80,768]{2,1,0:T(8,128)(2,1)} %get-tuple-element.32), channel_id=1, source_target_pairs={{0,1},{1,0},{2,3},{3,2},{4,5},{5,4},{6,7},{7,6},{8,9},{9,8},{10,11... | collective-permute-start | bytes 2949128 | tf_op jit(solution)/shard_map/ppermute | solution.py:29
  68.1 7.3 %copy-start.7 = (bf16[1,640,1024]{2,1,0:T(8,128)(2,1)S(1)}, bf16[1,640,1024]{2,1,0:T(8,128)(2,1)}, u32[]{:S(2)}) copy-start(bf16[1,640,1024]{2,1,0:T(8,128)(2,1)} %param.21) | copy-start | bytes 3932164
  68.1 7.3 %copy-start.9 = (bf16[1,640,1024]{2,1,0:T(8,128)(2,1)S(1)}, bf16[1,640,1024]{2,1,0:T(8,128)(2,1)}, u32[]{:S(2)}) copy-start(bf16[1,640,1024]{2,1,0:T(8,128)(2,1)} %param.20) | copy-start | bytes 3932164
  68.2 20.9 %collective-permute-start.25 = (bf16[4,1,1,128,768]{4,3,2,1,0:T(8,128)(2,1)S(1)}, bf16[4,1,1,128,768]{4,3,2,1,0:T(8,128)(2,1)S(1)}, u32[]{:S(2)}, u32[]{:S(2)}) collective-permute-start(bf16[4,1,1,128,768]{4,3,2,1,0:T(8,128)(2,1)S(1)} %pad_maximum_fusion.refs_0_.refs_2_.refs_4_.refs_6_), channel_id=1, source_target_pairs={{0,4},{1,5},{2,6},{3,7},{4,0},{5,1},{6,2},{7,3},{8,12},{9,13},{10,... | collective-permute-start | bytes 2359304 | tf_op jit(solution)/shard_map/ppermute | solution.py:29
  70.9 19.7 %collective-permute-start.26 = (bf16[4,1,1,128,768]{4,3,2,1,0:T(8,128)(2,1)S(1)}, bf16[4,1,1,128,768]{4,3,2,1,0:T(8,128)(2,1)S(1)}, u32[]{:S(2)}, u32[]{:S(2)}) collective-permute-start(bf16[4,1,1,128,768]{4,3,2,1,0:T(8,128)(2,1)S(1)} %pad_maximum_fusion.refs_0_.refs_2_.refs_4_.refs_6_), channel_id=1, source_target_pairs={{0,2},{1,3},{2,0},{3,1},{4,6},{5,7},{6,4},{7,5},{8,10},{9,11},{10,... | collective-permute-start | bytes 2359304 | tf_op jit(solution)/shard_map/ppermute | solution.py:29
  91.5 19.0 %collective-permute-start.27 = (bf16[2,1,1,128,768]{4,3,2,1,0:T(8,128)(2,1)S(1)}, bf16[2,1,1,128,768]{4,3,2,1,0:T(8,128)(2,1)S(1)}, u32[]{:S(2)}, u32[]{:S(2)}) collective-permute-start(bf16[2,1,1,128,768]{4,3,2,1,0:T(8,128)(2,1)S(1)} %slice.125), channel_id=1, source_target_pairs={{0,4},{1,5},{2,6},{3,7},{4,0},{5,1},{6,2},{7,3},{8,12},{9,13},{10,... | collective-permute-start | bytes 1179656 | tf_op jit(solution)/shard_map/ppermute | solution.py:29
  91.9 18.5 %collective-permute-start.28 = (bf16[2,1,1,128,768]{4,3,2,1,0:T(8,128)(2,1)S(1)}, bf16[2,1,1,128,768]{4,3,2,1,0:T(8,128)(2,1)S(1)}, u32[]{:S(2)}, u32[]{:S(2)}) collective-permute-start(bf16[2,1,1,128,768]{4,3,2,1,0:T(8,128)(2,1)S(1)} %slice.126), channel_id=1, source_target_pairs={{0,2},{1,3},{2,0},{3,1},{4,6},{5,7},{6,4},{7,5},{8,10},{9,11},{10,... | collective-permute-start | bytes 1179656 | tf_op jit(solution)/shard_map/ppermute | solution.py:29
  110.5 16.3 %collective-permute-start.31 = (bf16[8,128,768]{2,1,0:T(8,128)(2,1)}, bf16[8,128,768]{2,1,0:T(8,128)(2,1)S(1)}, u32[]{:S(2)}, u32[]{:S(2)}) collective-permute-start(bf16[8,128,768]{2,1,0:T(8,128)(2,1)} %bitcast.51), channel_id=1, source_target_pairs={{0,1},{1,0},{2,3},{3,2},{4,5},{5,4},{6,7},{7,6},{8,9},{9,8},{10,11... | collective-permute-start | bytes 4718600 | tf_op jit(solution)/shard_map/ppermute | solution.py:29
  126.2 3.3 %copy-start = (bf16[8,160,128]{2,1,0:T(8,128)(2,1)S(1)}, bf16[8,160,128]{2,1,0:T(8,128)(2,1)}, u32[]{:S(2)}) copy-start(bf16[8,160,128]{2,1,0:T(8,128)(2,1)} %add_convert_fusion.9.refs_8_) | copy-start | bytes 983044
  126.2 3.3 %copy-start.1 = (s32[32]{0:T(128)S(1)}, s32[32]{0:T(128)}, u32[]{:S(2)}) copy-start(s32[32]{0:T(128)} %convert_element_type.338.pid_ref) | copy-start | bytes 388
  126.2 3.3 %copy-start.3 = (s32[2]{0:T(128)S(1)}, s32[2]{0:T(128)}, u32[]{:S(2)}) copy-start(s32[2]{0:T(128)} %pad_add_fusion.2.my_ref) | copy-start | bytes 28
  126.2 13.6 %collective-permute-start.29 = (bf16[8,128,768]{2,1,0:T(8,128)(2,1)S(1)}, bf16[8,128,768]{2,1,0:T(8,128)(2,1)S(1)}, u32[]{:S(2)}, u32[]{:S(2)}) collective-permute-start(bf16[8,128,768]{2,1,0:T(8,128)(2,1)S(1)} %bitcast.219), channel_id=1, source_target_pairs={{0,1},{1,0},{2,3},{3,2},{4,5},{5,4},{6,7},{7,6},{8,9},{9,8},{10,11... | collective-permute-start | bytes 4718600 | tf_op jit(solution)/shard_map/ppermute | solution.py:29
  126.8 1.9 %copy-start.4 = (bf16[8,128,768]{2,1,0:T(8,128)(2,1)}, bf16[8,128,768]{2,1,0:T(8,128)(2,1)S(1)}, u32[]{:S(2)}) copy-start(bf16[8,128,768]{2,1,0:T(8,128)(2,1)S(1)} %collective-permute-done.31) | copy-start | bytes 4718596
  126.9 11.1 %collective-permute-start.32 = (bf16[4,64,768]{2,1,0:T(8,128)(2,1)S(1)}, bf16[4,64,768]{2,1,0:T(8,128)(2,1)S(1)}, u32[]{:S(2)}, u32[]{:S(2)}) collective-permute-start(bf16[4,64,768]{2,1,0:T(8,128)(2,1)S(1)} %fusion.34), channel_id=1, source_target_pairs={{0,4},{1,5},{2,6},{3,7},{4,0},{5,1},{6,2},{7,3},{8,12},{9,13},{10,... | collective-permute-start | bytes 1179656 | tf_op jit(solution)/shard_map/ppermute | solution.py:29
  128.6 2.2 %copy-start.2 = (s32[2]{0:T(128)S(1)}, s32[2]{0:T(128)}, u32[]{:S(2)}) copy-start(s32[2]{0:T(128)} %pad_add_fusion.1.my_ref) | copy-start | bytes 28
  128.6 20.5 %collective-permute-start.34 = (bf16[4,2,64,768]{3,2,0,1:T(8,128)(2,1)S(1)}, bf16[4,2,64,768]{3,2,0,1:T(8,128)(2,1)S(1)}, u32[]{:S(2)}, u32[]{:S(2)}) collective-permute-start(bf16[4,2,64,768]{3,2,0,1:T(8,128)(2,1)S(1)} %add_convert_fusion), channel_id=1, source_target_pairs={{0,2},{1,3},{2,0},{3,1},{4,6},{5,7},{6,4},{7,5},{8,10},{9,11},{10,... | collective-permute-start | bytes 2359304 | tf_op jit(solution)/shard_map/ppermute | solution.py:29
  130.7 26.8 %collective-permute-start.39 = (bf16[8,80,768]{2,1,0:T(8,128)(2,1)S(1)}, bf16[8,80,768]{2,1,0:T(8,128)(2,1)S(1)}, u32[]{:S(2)}, u32[]{:S(2)}) collective-permute-start(bf16[8,80,768]{2,1,0:T(8,128)(2,1)S(1)} %get-tuple-element.44), channel_id=1, source_target_pairs={{0,1},{1,0},{2,3},{3,2},{4,5},{5,4},{6,7},{7,6},{8,9},{9,8},{10,11... | collective-permute-start | bytes 2949128 | tf_op jit(solution)/shard_map/ppermute | solution.py:29
  130.8 19.2 %copy-start.8 = (bf16[1,640,1024]{2,1,0:T(8,128)(2,1)S(1)}, bf16[1,640,1024]{2,1,0:T(8,128)(2,1)}, u32[]{:S(2)}) copy-start(bf16[1,640,1024]{2,1,0:T(8,128)(2,1)} %param.21) | copy-start | bytes 3932164
  130.8 19.2 %copy-start.10 = (bf16[1,640,1024]{2,1,0:T(8,128)(2,1)S(1)}, bf16[1,640,1024]{2,1,0:T(8,128)(2,1)}, u32[]{:S(2)}) copy-start(bf16[1,640,1024]{2,1,0:T(8,128)(2,1)} %param.20) | copy-start | bytes 3932164
  132.1 17.9 %copy-start.6 = (bf16[8,80,3072]{2,1,0:T(8,128)(2,1)S(1)}, bf16[8,80,3072]{2,1,0:T(8,128)(2,1)}, u32[]{:S(2)}) copy-start(bf16[8,80,3072]{2,1,0:T(8,128)(2,1)} %constant_dynamic-update-slice_fusion.2) | copy-start | bytes 11796484
  132.1 25.5 %collective-permute-start.40 = (bf16[8,80,768]{2,1,0:T(8,128)(2,1)S(1)}, bf16[8,80,768]{2,1,0:T(8,128)(2,1)S(1)}, u32[]{:S(2)}, u32[]{:S(2)}) collective-permute-start(bf16[8,80,768]{2,1,0:T(8,128)(2,1)S(1)} %get-tuple-element.45), channel_id=1, source_target_pairs={{0,1},{1,0},{2,3},{3,2},{4,5},{5,4},{6,7},{7,6},{8,9},{9,8},{10,11... | collective-permute-start | bytes 2949128 | tf_op jit(solution)/shard_map/ppermute | solution.py:29
  139.1 18.7 %collective-permute-start.33 = (bf16[4,64,768]{2,1,0:T(8,128)(2,1)S(1)}, bf16[4,64,768]{2,1,0:T(8,128)(2,1)S(1)}, u32[]{:S(2)}, u32[]{:S(2)}) collective-permute-start(bf16[4,64,768]{2,1,0:T(8,128)(2,1)S(1)} %fusion.29), channel_id=1, source_target_pairs={{0,2},{1,3},{2,0},{3,1},{4,6},{5,7},{6,4},{7,5},{8,10},{9,11},{10,... | collective-permute-start | bytes 1179656 | tf_op jit(solution)/shard_map/ppermute | solution.py:29
  139.9 17.9 %collective-permute-start.30 = (bf16[4,64,768]{2,1,0:T(8,128)(2,1)S(1)}, bf16[4,64,768]{2,1,0:T(8,128)(2,1)S(1)}, u32[]{:S(2)}, u32[]{:S(2)}) collective-permute-start(bf16[4,64,768]{2,1,0:T(8,128)(2,1)S(1)} %fusion.32), channel_id=1, source_target_pairs={{0,4},{1,5},{2,6},{3,7},{4,0},{5,1},{6,2},{7,3},{8,12},{9,13},{10,... | collective-permute-start | bytes 1179656 | tf_op jit(solution)/shard_map/ppermute | solution.py:29
  149.3 9.0 %collective-permute-start.35 = (bf16[4,64,768]{2,1,0:T(8,128)(2,1)S(1)}, bf16[4,64,768]{2,1,0:T(8,128)(2,1)S(1)}, u32[]{:S(2)}, u32[]{:S(2)}) collective-permute-start(bf16[4,64,768]{2,1,0:T(8,128)(2,1)S(1)} %fusion.36), channel_id=1, source_target_pairs={{0,4},{1,5},{2,6},{3,7},{4,0},{5,1},{6,2},{7,3},{8,12},{9,13},{10,... | collective-permute-start | bytes 1179656 | tf_op jit(solution)/shard_map/ppermute | solution.py:29
  157.8 2.3 %copy-start.21 = (bf16[640,1024]{1,0:T(8,128)(2,1)S(1)}, bf16[640,1024]{1,0:T(8,128)(2,1)}, u32[]{:S(2)}) copy-start(bf16[640,1024]{1,0:T(8,128)(2,1)} %get-tuple-element.38.da) | copy-start | bytes 3932164
  158.8 9.2 %collective-permute-start.36 = (bf16[128,768]{1,0:T(8,128)(2,1)S(1)}, bf16[128,768]{1,0:T(8,128)(2,1)S(1)}, u32[]{:S(2)}, u32[]{:S(2)}) collective-permute-start(bf16[128,768]{1,0:T(8,128)(2,1)S(1)} %pad_maximum_fusion.2), channel_id=1, source_target_pairs={{0,8},{1,9},{2,10},{3,11},{4,12},{5,13},{6,14},{7,15},{8,0},{9,1},... | collective-permute-start | bytes 589832 | tf_op jit(solution)/shard_map/ppermute | solution.py:29
  160.1 10.4 %copy-start.20 = (bf16[640,1024]{1,0:T(8,128)(2,1)S(1)}, bf16[640,1024]{1,0:T(8,128)(2,1)}, u32[]{:S(2)}) copy-start(bf16[640,1024]{1,0:T(8,128)(2,1)} %get-tuple-element.39.db) | copy-start | bytes 3932164
  167.2 10.4 %collective-permute-start.38 = (bf16[128,768]{1,0:T(8,128)(2,1)S(1)}, bf16[128,768]{1,0:T(8,128)(2,1)S(1)}, u32[]{:S(2)}, u32[]{:S(2)}) collective-permute-start(bf16[128,768]{1,0:T(8,128)(2,1)S(1)} %pad_maximum_fusion.3), channel_id=1, source_target_pairs={{0,8},{1,9},{2,10},{3,11},{4,12},{5,13},{6,14},{7,15},{8,0},{9,1},... | collective-permute-start | bytes 589832 | tf_op jit(solution)/shard_map/ppermute | solution.py:29
  168.1 9.5 %collective-permute-start.37 = (bf16[128,768]{1,0:T(8,128)(2,1)S(1)}, bf16[128,768]{1,0:T(8,128)(2,1)S(1)}, u32[]{:S(2)}, u32[]{:S(2)}) collective-permute-start(bf16[128,768]{1,0:T(8,128)(2,1)S(1)} %add_convert_fusion.11), channel_id=1, source_target_pairs={{0,16},{1,17},{2,18},{3,19},{4,20},{5,21},{6,22},{7,23},{8,24},{9,... | collective-permute-start | bytes 589832 | tf_op jit(solution)/shard_map/ppermute | solution.py:29
